TPU v7x, 128 devices: a whole 4x4x4 slice. The times are simulated.
128 devices in a mesh: tracer: 2 (over core), gx: 8 (over z, x_lo), gy: 8 (over x_hi, y).
Axes of the slice: x: 4 (x_hi: 2, x_lo: 2; x = x_hi * 2 + x_lo), y: 4, z: 4, core: 2. Of those that a mesh axis runs over, the one named last changes fastest.
Arguments:
- tracers: float32 [8, 16, 1024, 1024], P('tracer', None, 'gx', 'gy'), may hold values from -6 to 6
- wind_east: float32 [16, 1024, 1024], P(None, 'gx', 'gy'), may hold values from -0.2 to 0.2
- wind_north: float32 [16, 1024, 1024], P(None, 'gx', 'gy'), may hold values from -0.2 to 0.2
- diffusivity: float32 [16, 1024, 1024], P(None, 'gx', 'gy'), may hold values from 0.02 to 0.08
- emission: float32 [1024, 1024], P('gx', 'gy'), may hold values from 0.1 to 3
- region_tag: int32 [1024, 1024], P('gx', 'gy'), may hold values from 0 to 7
- footprint: float32 [8192, 80], P(('gx', 'gy')), may hold values from -4 to 4
- corners: int32 [8192, 2], P(('gx', 'gy')), may hold values from 0 to 992, as said below
- owner_map: int32 [64], replicated, may hold values from 0 to 63, each once
Outputs:
- stepped: float32 [8, 16, 1024, 1024], P('tracer', None, 'gx', 'gy')
- observed: float32 [8, 8192], P('tracer', ('gx', 'gy'))
Inputs may be any that keep to these rules, and one draw needn't show every extreme that they name: Each observation's footprint lies inside the grid: corners[:, 0] <= 992 and corners[:, 1] <= 992. owner_map is a permutation.
All inputs are finite; a program needn't handle non-finite values.
Results may differ from a plain program's by a relative error of at most 0.0049.
Values sent between devices are 32-bit elements; how exact they have to be, the bound alone decides.
No kernel may reach another device: no remote copies, remote signals or barrier semaphores. Data moves between devices by JAX's collectives and lax.ppermute only.
A program may use at most 192 MiB of HBM per device.

v0:
```python
import math

import jax
import jax.numpy as jnp
from jax import lax
from jax.sharding import PartitionSpec as P

NZ = 16
FP = 32


def padded_2(cells, sides, width):
    for axis, dim in sides:
        count = lax.axis_size(axis)
        ends = count - 1
        head = lax.slice_in_dim(cells, 0, width, axis=dim)
        tail = lax.slice_in_dim(cells, cells.shape[dim] - width, cells.shape[dim], axis=dim)
        cells = jnp.concatenate(
            [
                lax.ppermute(tail, axis, [(i, (i + 1) % count) for i in range(ends)]),
                cells,
                lax.ppermute(head, axis, [((i + 1) % count, i) for i in range(ends)]),
            ],
            axis=dim,
        )
    return cells


def face_flux(left, right, wind, kleft, kright):
    return (
        jnp.maximum(wind, 0.0) * left
        + jnp.minimum(wind, 0.0) * right
        - 0.5 * (kleft + kright) * (right - left)
    )


def per_device(
    tracers, wind_east, wind_north, diffusivity, emission, region_tag, footprint, corners, owner_map
):
    local_count = tracers.shape[0]
    cols_x = tracers.shape[2]
    cols_y = tracers.shape[3]
    fields = jnp.concatenate(
        [tracers, wind_east[None], wind_north[None], diffusivity[None]], axis=0
    )
    padded = padded_2(fields, (("gx", 2), ("gy", 3)), 1)
    conc = padded[:local_count]
    pad_east = padded[local_count][None]
    pad_north = padded[local_count + 1][None]
    pad_diff = padded[local_count + 2][None]
    flux_x = face_flux(
        conc[:, :, :-1, 1:-1],
        conc[:, :, 1:, 1:-1],
        pad_east[:, :, :-1, 1:-1],
        pad_diff[:, :, :-1, 1:-1],
        pad_diff[:, :, 1:, 1:-1],
    )
    flux_y = face_flux(
        conc[:, :, 1:-1, :-1],
        conc[:, :, 1:-1, 1:],
        pad_north[:, :, 1:-1, :-1],
        pad_diff[:, :, 1:-1, :-1],
        pad_diff[:, :, 1:-1, 1:],
    )
    stepped = (
        tracers
        - (flux_x[:, :, 1:] - flux_x[:, :, :-1])
        - (flux_y[:, :, :, 1:] - flux_y[:, :, :, :-1])
    )
    tracer_ids = lax.axis_index("tracer") * local_count + jnp.arange(local_count, dtype=jnp.int32)
    tagged = (tracer_ids[:, None, None] == region_tag[None]).astype(jnp.float32)
    stepped = stepped.at[:, 0].add(emission[None] * tagged)
    rounded = stepped.astype(jnp.bfloat16)
    east_first = lax.axis_index("gx") * cols_x
    north_first = lax.axis_index("gy") * cols_y
    east_cols = east_first + jnp.arange(cols_x, dtype=jnp.int32)
    north_cols = north_first + jnp.arange(cols_y, dtype=jnp.int32)
    obs_scale = 1.0 / (FP * math.sqrt(NZ))

    def profile(prof, first, columns):
        offset = columns[None, :] - first[:, None]
        inside = (offset >= 0) & (offset < FP)
        chosen = jnp.take_along_axis(prof, jnp.clip(offset, 0, FP - 1), axis=1)
        return jnp.where(inside, chosen, 0.0).astype(jnp.bfloat16)

    def block_terms(items):
        rows, firsts = items
        weight_x = profile(rows[:, :FP], firsts[:, 0], east_cols)
        weight_y = profile(rows[:, FP : 2 * FP], firsts[:, 1], north_cols).astype(jnp.float32)
        kernel = rows[:, 2 * FP :]
        partly = jnp.einsum("ox,tzxy->tzoy", weight_x, rounded, preferred_element_type=jnp.float32)
        summed_y = jnp.einsum("tzoy,oy->tzo", partly, weight_y, precision=lax.Precision.HIGHEST)
        return (
            jnp.einsum("tzo,oz->to", summed_y, kernel, precision=lax.Precision.HIGHEST) * obs_scale
        )

    block_count = lax.axis_size("gx") * lax.axis_size("gy")
    obs_block = footprint.shape[0]
    holder = (
        jnp.zeros((block_count,), jnp.int32)
        .at[owner_map]
        .set(jnp.arange(block_count, dtype=jnp.int32))
    )
    rows, firsts = lax.all_gather((footprint, corners), ("gx", "gy"), axis=0, tiled=True)
    count = rows.shape[0]
    start_x = firsts[:, 0]
    start_y = firsts[:, 1]
    touches = (
        (start_x < east_first + cols_x)
        & (start_x + FP > east_first)
        & (start_y < north_first + cols_y)
        & (start_y + FP > north_first)
    )
    order = jnp.argsort(jnp.where(touches, 0, 1).astype(jnp.int32), stable=True)
    live = jnp.sum(touches.astype(jnp.int32))
    block_rows = min(128, count)
    rounds = (live + block_rows - 1) // block_rows

    def one_round(step, acc):
        begin = jnp.minimum(step * block_rows, count - block_rows).astype(jnp.int32)
        taken = lax.dynamic_slice_in_dim(order, begin, block_rows)
        terms = block_terms((rows[taken], firsts[taken]))
        return acc.at[:, taken].set(terms)

    empty = jnp.zeros((local_count, count), jnp.float32)
    terms = lax.fori_loop(jnp.zeros((), jnp.int32), rounds, one_round, empty)
    observed = lax.psum_scatter(
        terms.reshape(local_count, block_count, obs_block)[:, holder].reshape(
            local_count, block_count * obs_block
        ),
        ("gx", "gy"),
        scatter_dimension=1,
        tiled=True,
    )
    return (stepped, observed)


def solution(mesh):
    return jax.shard_map(
        per_device,
        mesh=mesh,
        in_specs=(
            P("tracer", None, "gx", "gy"),
            P(None, "gx", "gy"),
            P(None, "gx", "gy"),
            P(None, "gx", "gy"),
            P("gx", "gy"),
            P("gx", "gy"),
            P(("gx", "gy"), None),
            P(("gx", "gy"), None),
            P(),
        ),
        out_specs=(P("tracer", None, "gx", "gy"), P("tracer", ("gx", "gy"))),
        check_vma=False,
    )
```

profile of v0, /device:TPU:0, one launch (start us, length us, event | category | flops | bytes accessed | tf_op | source)
XLA Modules:
  0.0 2222.7 jit_solution(18350284538747050520)
XLA Ops:
  7.2 1.8 copy.80
  9.1 5.0 copy.51
  14.1 1.2 copy_bitcast_fusion
  16.1 1.4 collective-permute-start.1
  17.6 4.5 collective-permute-start
  22.1 0.7 copy.56
  22.9 176.3 %all_gather.6 = s32[8192,2]{0,1:T(2,128)S(1)} all-gather(s32[128,2]{0,1:T(2,128)S(1)} %copy-done.17), channel_id=1, replica_groups=mesh['tracer'=2,'gx'=8,'gy'=8] {'gx','gy'}, dimensions={0}, use_global_device_ids=true | all-gather | bytes 66560 | tf_op jit(solution)/shard_map/all_gather | solution.py:104
  200.6 2.7 copy.57
  203.3 1.0 scatter_custom_fusion.1
  204.9 6.8 sort.17
  211.7 5.0 pad_maximum_fusion.1
  216.7 12.5 fusion.56
  229.2 7.6 copy.52
  236.8 1.9 collective-permute-start.2
  238.7 7.0 copy.54
  245.7 1.6 collective-permute-start.3
  247.9 20.8 maximum_maximum_fusion.1
  268.7 3.2 multiply_subtract_fusion.1
  271.9 6.9 copy.53
  278.8 3.2 maximum_bitcast_fusion
  282.0 1.6 minimum_bitcast_fusion
  283.6 6.2 copy.55
  289.9 3.9 fusion.49
  293.8 1.6 slice-done.1
  296.2 2.2 copy-done.9
  298.4 16.5 maximum_maximum_fusion
  314.9 9.3 multiply_subtract_fusion
  324.2 4.0 fusion.46
  328.3 2.0 copy-done.10
  330.6 8.3 scatter-add.4
  338.9 2.5 convert_element_type.15
  341.9 18.9 all-gather.2.cloned.1.call-done
  360.8 2.3 broadcast_in_dim.47
  363.1 305.5 %while.12 = (s32[]{:T(128)}, f32[4,8192]{0,1:T(8,128)}, s32[]{:T(128)}, s32[8192]{0:T(1024)S(1)}, f32[8192,80]{1,0:T(8,128)}, /*index=5*/s32[8192,2]{1,0:T(8,128...) while((s32[]{:T(128)}, f32[4,8192]{0,1:T(8,128)}, ...), condition=%wide.region_4.6_spmd.clone, body=%wide.region_2.5_spmd.clone.sunk | while | flops 281872512 | bytes 11561179 | solution.py:126
  363.2 2.8 gather_fusion
  366.2 2.8 gather_fusion.1
  369.3 136.7 %gather_fusion.2 = bf16[16384]{0:T(1024)(128)(2,1)S(1)} fusion(bf16[128,32]{1,0:T(8,128)(2,1)S(1)} %get-tuple-element.227, s32[16384]{0:T(1024)S(1)} %fusion.82), kind=kCustom, calls=%fused_computation.1.clone.clone.1 | custom fusion | bytes 196608 | tf_op jit(solution)/shard_map/while/body/jit(take_along_axis)/gather | solution.py:83
  506.0 2.7 convolution_bitcast_fusion.2
  508.8 136.7 %gather_fusion.3 = bf16[16384]{0:T(1024)(128)(2,1)S(1)} fusion(bf16[128,32]{1,0:T(8,128)(2,1)S(1)} %get-tuple-element.230, s32[16384]{0:T(1024)S(1)} %fusion.83), kind=kCustom, calls=%fused_computation.clone.clone.1 | custom fusion | bytes 196608 | tf_op jit(solution)/shard_map/while/body/jit(take_along_axis)/gather | solution.py:83
  645.6 16.9 fusion.85
  662.6 1.0 fusion.86
  663.6 5.0 scatter_custom_fusion.8
  668.6 2.8 copy.60
  671.4 0.8 gather_fusion.4
  672.2 2.6 copy.70
  674.9 5.5 copy.61
  680.4 1533.8 %reduce-scatter.4.cloned.1.call-done = f32[128,4]{1,0:T(8,128)} async-done(((f32[8192,4]{1,0:T(8,128)}), f32[128,4]{1,0:T(8,128)}) %reduce-scatter.4.cloned.1.call-update) | async-done | bytes 2064
  2214.2 1.5 copy.71
  (75 shorter events, 5.4 us)
Async XLA Ops:
  7.2 353.7 %all-gather.2.cloned.1.call-start = ((), (), s32[]{:S(2)}) async-start(), calls=%async_computation.1 | async-start | bytes 4259840 | tf_op jit(solution)/shard_map/all_gather | solution.py:104
  9.0 269.7 %copy-start.3 = (f32[16,128,128]{2,0,1:T(8,128)}, f32[16,128,128]{2,0,1:T(8,128)S(1)}, u32[]{:S(2)}) copy-start(f32[16,128,128]{2,0,1:T(8,128)S(1)} %copy.80) | copy-start | bytes 3145732
  9.1 5.1 copy-start.12
  9.1 5.1 copy-start.13
  14.1 2.0 copy-start
  15.4 263.4 %copy-start.5 = (f32[1,16,128,128]{3,1,2,0:T(8,128)}, f32[1,16,128,128]{3,1,2,0:T(8,128)S(1)}, u32[]{:S(2)}) copy-start(f32[1,16,128,128]{3,1,2,0:T(8,128)S(1)} %get-tuple-element.162) | copy-start | bytes 3145732
  15.4 263.4 %copy-start.7 = (f32[1,16,128,128]{3,1,2,0:T(8,128)}, f32[1,16,128,128]{3,1,2,0:T(8,128)S(1)}, u32[]{:S(2)}) copy-start(f32[1,16,128,128]{3,1,2,0:T(8,128)S(1)} %get-tuple-element.163) | copy-start | bytes 3145732
  15.4 6.7 copy-start.16
  15.4 7.5 copy-start.17
  16.1 187.2 %copy-start.18 = (s32[64]{0:T(128)S(1)}, s32[64]{0:T(128)}, u32[]{:S(2)}) copy-start(s32[64]{0:T(128)} %param.23) | copy-start | bytes 772
  16.1 195.5 %collective-permute-start.1 = (f32[7,16,1,128]{3,1,2,0:T(8,128)S(1)}, f32[7,16,1,128]{3,1,2,0:T(8,128)S(1)}, u32[]{:S(2)}, u32[]{:S(2)}) collective-permute-start(f32[7,16,1,128]{3,1,2,0:T(8,128)S(1)} %get-tuple-element.161), channel_id=1, source_target_pairs={{8,0},{16,8},{24,16},{32,24},{40,32},{48,40},{56,48},{9,1},{17,9},... | collective-permute-start | bytes 172040 | tf_op jit(solution)/shard_map/ppermute | solution.py:22
  17.6 194.1 %collective-permute-start = (f32[7,16,1,128]{3,1,2,0:T(8,128)S(1)}, f32[7,16,1,128]{3,1,2,0:T(8,128)S(1)}, u32[]{:S(2)}, u32[]{:S(2)}) collective-permute-start(f32[7,16,1,128]{3,1,2,0:T(8,128)S(1)} %get-tuple-element.160), channel_id=1, source_target_pairs={{0,8},{8,16},{16,24},{24,32},{32,40},{40,48},{48,56},{1,9},{9,17},... | collective-permute-start | bytes 172040 | tf_op jit(solution)/shard_map/ppermute | solution.py:20
  22.9 2191.3 %reduce-scatter.4.cloned.1.call-start = ((), (), s32[]{:S(2)}) async-start(), calls=%async_computation.2 | async-start | bytes 4259840
  236.8 35.1 %collective-permute-start.2 = (f32[7,16,130,1]{2,1,3,0:T(8,128)}, f32[7,16,130,1]{2,1,3,0:T(8,128)}, u32[]{:S(2)}, u32[]{:S(2)}) collective-permute-start(f32[7,16,130,1]{2,1,3,0:T(8,128)} %copy.52), channel_id=1, source_target_pairs={{0,1},{1,2},{2,3},{3,4},{4,5},{5,6},{6,7},{8,9},{9,10},{10,11},{11... | collective-permute-start | bytes 174728 | tf_op jit(solution)/shard_map/ppermute | solution.py:20
  245.7 2.2 copy-start.1
  245.7 37.9 %collective-permute-start.3 = (f32[7,16,130,1]{2,1,3,0:T(8,128)S(1)}, f32[7,16,130,1]{2,1,3,0:T(8,128)S(1)}, u32[]{:S(2)}, u32[]{:S(2)}) collective-permute-start(f32[7,16,130,1]{2,1,3,0:T(8,128)S(1)} %copy.54), channel_id=1, source_target_pairs={{1,0},{2,1},{3,2},{4,3},{5,4},{6,5},{7,6},{9,8},{10,9},{11,10},{12... | collective-permute-start | bytes 174728 | tf_op jit(solution)/shard_map/ppermute | solution.py:22
  283.6 10.2 slice-start
  289.9 3.9 copy-start.2
  289.9 5.5 slice-start.1
  289.9 5.7 copy-start.4
  289.9 6.0 copy-start.6
  289.9 6.3 copy-start.8
  289.9 8.5 copy-start.9
  289.9 34.3 %slice-start.2 = ((s8[4227072]{0:T(1024)(128)(4,1)}), s8[4194304]{0:T(1024)(128)(4,1)S(1)}, s32[]{:S(2)}) async-start(s8[4227072]{0:T(1024)(128)(4,1)} %bitcast.119), calls=%async_computation.5 | async-start | bytes 8388608
  298.4 25.8 %slice-start.3 = ((s8[4227072]{0:T(1024)(128)(4,1)}), s8[32768]{0:T(1024)(128)(4,1)S(1)}, s32[]{:S(2)}) async-start(s8[4227072]{0:T(1024)(128)(4,1)} %bitcast.119), calls=%async_computation.6 | async-start | bytes 65536
  314.9 9.3 copy-start.11
  324.2 6.1 copy-start.14
  324.2 6.1 copy-start.15
  328.3 2.0 copy-start.10
Sparse Core Ops, SparseCore 0:
  23.0 337.7 all-gather.1
  675.0 1539.1 reduce-scatter.3
where the time goes:
time: 2230 us; the launch traced here: 2220 us
  waiting for transfers between devices  1550 us (70%)
  local copies, waits for them, and re-layouts  364 us (16%)
  blocking collectives  176 us (8%)
  other arithmetic  84.2 us (4%)
    unnamed x3, waiting for transfers between devices  1530 us
    gather x2, local copies, waits for them, and re-layouts, profile(): chosen = jnp.take_along_axis(prof, jnp.clip(offset, 0, FP - 1), axis=1)  273 us
    all_gather x1, blocking collectives, per_device(): lax.all_gather((footprint, corners), ('gx', 'gy'), axis=0, tiled=True)  176 us
  transfers between devices with their start and end apart: 6, of which 2 were waited for; matrix products, arithmetic and copies ran while one was open for 6% of the time, Pallas kernels for 0%

commit v1 on v0

v1 whole, which is shorter than its diff:
```python
import functools
import math

import jax
import jax.numpy as jnp
from jax import lax
from jax.experimental import pallas as pl
from jax.experimental.pallas import tpu as pltpu
from jax.sharding import PartitionSpec as P

FP = 32
CAP = 24
LANES = 128
TILES = ("gx", "gy")


def edges_kernel(nz, c_ref, we_ref, wn_ref, k_ref, e_ref, w_ref, n_ref, s_ref):
    count, zb = c_ref.shape[0], c_ref.shape[1]
    cols_x, cols_y = c_ref.shape[2], c_ref.shape[3]
    step = pl.program_id(0)

    @pl.when(step == 0)
    def _():
        n_ref[...] = jnp.zeros_like(n_ref)
        s_ref[...] = jnp.zeros_like(s_ref)

    lane = lax.broadcasted_iota(jnp.int32, n_ref.shape, 1)
    north = n_ref[...]
    south = s_ref[...]
    for zi in range(zb):
        z = step * zb + zi
        for t in range(count):
            slot = t * nz + z
            cells = c_ref[t, zi]
            e_ref[pl.ds(slot, 1), :] = c_ref[t, zi, cols_x - 1 : cols_x, :]
            w_ref[pl.ds(slot, 1), :] = c_ref[t, zi, 0:1, :]
            north = jnp.where(lane == slot, pltpu.roll(cells, slot + 1, 1), north)
            south = jnp.where(lane == slot, pltpu.roll(cells, slot, 1), south)
        slot = count * nz + z
        cells = k_ref[zi]
        e_ref[pl.ds(slot, 1), :] = k_ref[zi, cols_x - 1 : cols_x, :]
        w_ref[pl.ds(slot, 1), :] = k_ref[zi, 0:1, :]
        north = jnp.where(lane == slot, pltpu.roll(cells, slot + 1, 1), north)
        south = jnp.where(lane == slot, pltpu.roll(cells, slot, 1), south)
        slot = (count + 1) * nz + z
        e_ref[pl.ds(slot, 1), :] = we_ref[zi, cols_x - 1 : cols_x, :]
        north = jnp.where(lane == slot, pltpu.roll(wn_ref[zi], slot + 1, 1), north)
    n_ref[...] = north
    s_ref[...] = south


def edges(tracers, wind_east, wind_north, diffusivity):
    count, nz, cols_x, cols_y = tracers.shape
    zb = 4
    level = pl.BlockSpec((zb, cols_x, cols_y), lambda i: (i, 0, 0))
    rows_e = (count + 2) * nz
    rows_w = (count + 1) * nz
    f32 = jnp.float32
    return pl.pallas_call(
        functools.partial(edges_kernel, nz),
        grid=(nz // zb,),
        in_specs=[
            pl.BlockSpec((count, zb, cols_x, cols_y), lambda i: (0, i, 0, 0)),
            level,
            level,
            level,
        ],
        out_specs=[
            pl.BlockSpec((rows_e, cols_y), lambda i: (0, 0)),
            pl.BlockSpec((rows_w, cols_y), lambda i: (0, 0)),
            pl.BlockSpec((cols_x, LANES), lambda i: (0, 0)),
            pl.BlockSpec((cols_x, LANES), lambda i: (0, 0)),
        ],
        out_shape=[
            jax.ShapeDtypeStruct((rows_e, cols_y), f32),
            jax.ShapeDtypeStruct((rows_w, cols_y), f32),
            jax.ShapeDtypeStruct((cols_x, LANES), f32),
            jax.ShapeDtypeStruct((cols_x, LANES), f32),
        ],
        name="edges",
    )(tracers, wind_east, wind_north, diffusivity)


def step_kernel(
    nz, first_ref, c_ref, we_ref, wn_ref, k_ref, em_ref, tag_ref,
    hw_ref, he_ref, hs_ref, hn_ref, out_ref, r_ref,
):
    count = c_ref.shape[0]
    cols_x, cols_y = c_ref.shape[2], c_ref.shape[3]
    z = pl.program_id(0)
    row = lax.broadcasted_iota(jnp.int32, (cols_x, cols_y), 0)
    lane = lax.broadcasted_iota(jnp.int32, (cols_x, cols_y), 1)
    row_lo, row_hi = row == 0, row == cols_x - 1
    lane_lo, lane_hi = lane == 0, lane == cols_y - 1

    def from_west(a, slot):
        return jnp.where(row_lo, hw_ref[pl.ds(slot, 1), :], pltpu.roll(a, 1, 0))

    def from_east(a, slot):
        return jnp.where(row_hi, he_ref[pl.ds(slot, 1), :], pltpu.roll(a, cols_x - 1, 0))

    def from_south(a, slot):
        edge = pltpu.roll(hs_ref[...], LANES - slot, 1)
        return jnp.where(lane_lo, edge, pltpu.roll(a, 1, 1))

    def from_north(a, slot):
        edge = pltpu.roll(hn_ref[...], LANES - 1 - slot, 1)
        return jnp.where(lane_hi, edge, pltpu.roll(a, cols_y - 1, 1))

    we, wn, k = we_ref[0], wn_ref[0], k_ref[0]
    at_k, at_w = count * nz + z, (count + 1) * nz + z
    d_e = 0.5 * (k + from_east(k, at_k))
    d_n = 0.5 * (k + from_north(k, at_k))
    d_w = 0.5 * (k + from_west(k, at_k))
    d_s = 0.5 * (k + from_south(k, at_k))
    we_m = from_west(we, at_w)
    wn_m = from_south(wn, at_w)
    a_e, b_e = jnp.maximum(we, 0.0) + d_e, jnp.minimum(we, 0.0) - d_e
    a_n, b_n = jnp.maximum(wn, 0.0) + d_n, jnp.minimum(wn, 0.0) - d_n
    a_w, b_w = jnp.maximum(we_m, 0.0) + d_w, jnp.minimum(we_m, 0.0) - d_w
    a_s, b_s = jnp.maximum(wn_m, 0.0) + d_s, jnp.minimum(wn_m, 0.0) - d_s
    middle = 1.0 - (a_e - b_w) - (a_n - b_s)
    for t in range(count):
        c = c_ref[t, 0]
        slot = t * nz + z
        new = (
            middle * c
            - b_e * from_east(c, slot)
            + a_w * from_west(c, slot)
            - b_n * from_north(c, slot)
            + a_s * from_south(c, slot)
        )
        out_ref[t, 0] = new

    @pl.when(z == 0)
    def _():
        for t in range(count):
            hit = tag_ref[...] == first_ref[0] + t
            out_ref[t, 0] = out_ref[t, 0] + jnp.where(hit, em_ref[...], 0.0)

    for t in range(count):
        r_ref[:, t * cols_y : (t + 1) * cols_y] = out_ref[t, 0].astype(jnp.bfloat16)


def advance(first, tracers, wind_east, wind_north, diffusivity, emission, tag, halos):
    count, nz, cols_x, cols_y = tracers.shape
    level = pl.BlockSpec((1, cols_x, cols_y), lambda z: (z, 0, 0))

    def whole(a):
        return pl.BlockSpec(a.shape, lambda z: (0, 0))

    fields = pl.BlockSpec((count, 1, cols_x, cols_y), lambda z: (0, z, 0, 0))
    return pl.pallas_call(
        functools.partial(step_kernel, nz),
        grid=(nz,),
        in_specs=[
            pl.BlockSpec(memory_space=pltpu.SMEM),
            fields,
            level,
            level,
            level,
            whole(emission),
            whole(tag),
            *[whole(h) for h in halos],
        ],
        out_specs=[fields, pl.BlockSpec((cols_x, count * cols_y), lambda z: (z, 0))],
        out_shape=[
            jax.ShapeDtypeStruct(tracers.shape, jnp.float32),
            jax.ShapeDtypeStruct((nz * cols_x, count * cols_y), jnp.bfloat16),
        ],
        cost_estimate=pl.CostEstimate(
            flops=40 * tracers.size, bytes_accessed=13 << 20, transcendentals=0
        ),
        name="advance",
    )(first, tracers, wind_east, wind_north, diffusivity, emission, tag, *halos)


def pack_kernel(tiles_x, tiles_y, size, nz, round_ref, fp_ref, corner_ref, corner_t_ref, out_ref, m_ref):
    tiles = tiles_x * tiles_y
    obs = fp_ref.shape[0]
    tile = lax.broadcasted_iota(jnp.int32, (tiles, obs), 0)
    first_x = (tile // tiles_y) * size[0]
    first_y = (tile % tiles_y) * size[1]
    x0 = corner_t_ref[0:1, :]
    y0 = corner_t_ref[1:2, :]
    touch = (
        (x0 < first_x + size[0])
        & (x0 + FP > first_x)
        & (y0 < first_y + size[1])
        & (y0 + FP > first_y)
    )
    ones = jnp.where(touch, 1.0, 0.0)
    before = lax.broadcasted_iota(jnp.int32, (obs, obs), 0) < lax.broadcasted_iota(
        jnp.int32, (obs, obs), 1
    )
    rank = jnp.dot(
        ones.astype(jnp.bfloat16),
        jnp.where(before, 1.0, 0.0).astype(jnp.bfloat16),
        preferred_element_type=jnp.float32,
    ).astype(jnp.int32)
    most = jnp.max(jnp.sum(ones, axis=1, keepdims=True), axis=0, keepdims=True)
    slot = jnp.where(touch, rank - round_ref[0] * CAP, -1)
    which = lax.broadcasted_iota(jnp.int32, (tiles, CAP, obs), 1)
    pick = jnp.where(slot[:, None, :] == which, 1.0, 0.0).reshape(tiles * CAP, obs)
    pick = pick.astype(jnp.bfloat16)

    width = 2 * FP + nz
    lane = lax.broadcasted_iota(jnp.int32, (obs, LANES), 1)
    m_ref[...] = jnp.zeros_like(m_ref)
    m_ref[:, 0:width] = fp_ref[...]
    corner = corner_ref[...].astype(jnp.float32)
    rows = m_ref[...]
    rows = jnp.where(lane == width, corner[:, 0:1], rows)
    rows = jnp.where(lane == width + 1, corner[:, 1:2], rows)
    rows = jnp.where(
        lane == width + 2,
        lax.broadcasted_iota(jnp.int32, (obs, LANES), 0).astype(jnp.float32),
        rows,
    )
    high = rows.astype(jnp.bfloat16)
    low = jnp.where(lane < 2 * FP, 0.0, rows - high.astype(jnp.float32)).astype(jnp.bfloat16)
    packed = jnp.dot(pick, high, preferred_element_type=jnp.float32) + jnp.dot(
        pick, low, preferred_element_type=jnp.float32
    )
    lane_all = lax.broadcasted_iota(jnp.int32, packed.shape, 1)
    packed = jnp.where(lane_all == width + 3, most, packed)
    out_ref[...] = packed


def pack(number, footprint, corners, tiles_x, tiles_y, size):
    obs, width = footprint.shape
    nz = width - 2 * FP
    tiles = tiles_x * tiles_y
    vmem = pl.BlockSpec(memory_space=pltpu.VMEM)
    return pl.pallas_call(
        functools.partial(pack_kernel, tiles_x, tiles_y, size, nz),
        in_specs=[pl.BlockSpec(memory_space=pltpu.SMEM), vmem, vmem, vmem],
        out_specs=vmem,
        out_shape=jax.ShapeDtypeStruct((tiles * CAP, LANES), jnp.float32),
        scratch_shapes=[pltpu.VMEM((obs, LANES), jnp.float32)],
        compiler_params=pltpu.CompilerParams(vmem_limit_bytes=32 << 20),
        name="pack",
    )(number, footprint, corners, corners.T)


def observe_kernel(nz, sources, origin_ref, owner_ref, rows_ref, r_ref, out_ref, most_ref, w_ref):
    count = out_ref.shape[1]
    cols = LANES
    group = 16
    chunk = group * CAP
    scale = 1.0 / (FP * math.sqrt(nz))
    width = 2 * FP + nz

    def body(step, most):
        rows = rows_ref[pl.ds(pl.multiple_of(step * chunk, chunk), chunk), :]
        lane = lax.broadcasted_iota(jnp.int32, (chunk, cols), 1)

        def along(at, place, origin):
            offset = lane - (rows[:, place : place + 1].astype(jnp.int32) - origin)
            inside = (offset >= 0) & (offset < FP)
            taken = jnp.take_along_axis(rows, jnp.clip(offset, 0, FP - 1) + at, axis=1)
            return jnp.where(inside, taken, 0.0)

        wx = along(0, width, origin_ref[0])
        wy = along(FP, width + 1, origin_ref[1]) * scale
        for z in range(nz):
            part = wx * rows[:, 2 * FP + z : 2 * FP + z + 1]
            w_ref[:, z * cols : (z + 1) * cols] = part.astype(jnp.bfloat16)
        got = jnp.dot(w_ref[...], r_ref[...], preferred_element_type=jnp.float32)
        mine = rows[:, width + 2 : width + 3].astype(jnp.int32) == lane
        for t in range(count):
            value = jnp.sum(got[:, t * cols : (t + 1) * cols] * wy, axis=1, keepdims=True)
            spread = jnp.where(mine, value, 0.0).reshape(group, CAP, cols)
            spread = jnp.sum(spread, axis=1)
            for g in range(group):
                out_ref[owner_ref[step * group + g], t : t + 1, :] = spread[g : g + 1, :]
        return jnp.maximum(most, jnp.max(rows[:, width + 3 : width + 4], axis=0, keepdims=True))

    most = lax.fori_loop(0, sources // group, body, jnp.zeros((1, 1), jnp.float32))
    most_ref[...] = jnp.broadcast_to(most, most_ref.shape).astype(jnp.int32)


def observe(origin, owner_map, rows, rounded, count, nz):
    sources = owner_map.shape[0]
    vmem = pl.BlockSpec(memory_space=pltpu.VMEM)
    smem = pl.BlockSpec(memory_space=pltpu.SMEM)
    return pl.pallas_call(
        functools.partial(observe_kernel, nz, sources),
        in_specs=[smem, smem, vmem, vmem],
        out_specs=[vmem, vmem],
        out_shape=[
            jax.ShapeDtypeStruct((sources, count, LANES), jnp.float32),
            jax.ShapeDtypeStruct((8, LANES), jnp.int32),
        ],
        scratch_shapes=[pltpu.VMEM((16 * CAP, rounded.shape[0]), jnp.bfloat16)],
        compiler_params=pltpu.CompilerParams(vmem_limit_bytes=48 << 20),
        name="observe",
    )(origin, owner_map, rows, rounded)


def per_device(
    tracers, wind_east, wind_north, diffusivity, emission, region_tag, footprint, corners, owner_map
):
    count, nz, cols_x, cols_y = tracers.shape
    tiles_x, tiles_y = lax.axis_size("gx"), lax.axis_size("gy")
    tiles = tiles_x * tiles_y
    obs = footprint.shape[0]

    east, west, north, south = edges(tracers, wind_east, wind_north, diffusivity)
    up_x = [(i, i + 1) for i in range(tiles_x - 1)]
    up_y = [(i, i + 1) for i in range(tiles_y - 1)]
    halos = (
        lax.ppermute(east, "gx", up_x),
        lax.ppermute(west, "gx", [(b, a) for a, b in up_x]),
        lax.ppermute(north, "gy", up_y),
        lax.ppermute(south, "gy", [(b, a) for a, b in up_y]),
    )
    first = (lax.axis_index("tracer") * count).astype(jnp.int32).reshape(1)
    stepped, rounded = advance(
        first, tracers, wind_east, wind_north, diffusivity, emission, region_tag, halos
    )
    origin = jnp.stack([lax.axis_index("gx") * cols_x, lax.axis_index("gy") * cols_y])
    origin = origin.astype(jnp.int32)

    def one_round(number):
        sent = pack(
            jnp.reshape(number, (1,)).astype(jnp.int32),
            footprint, corners, tiles_x, tiles_y, (cols_x, cols_y),
        )
        rows = lax.all_to_all(sent.reshape(tiles, CAP, LANES), TILES, 0, 0)
        parts, most = observe(
            origin, owner_map, rows.reshape(tiles * CAP, LANES), rounded, count, nz
        )
        parts = lax.all_to_all(parts, TILES, 0, 0)
        return jnp.sum(parts, axis=0), most[0, 0]

    observed, most = one_round(jnp.int32(0))
    rounds = (most + CAP - 1) // CAP
    observed = lax.fori_loop(
        jnp.int32(1), rounds, lambda r, total: total + one_round(r)[0], observed
    )
    return (stepped, observed)


def solution(mesh):
    return jax.shard_map(
        per_device,
        mesh=mesh,
        in_specs=(
            P("tracer", None, "gx", "gy"),
            P(None, "gx", "gy"),
            P(None, "gx", "gy"),
            P(None, "gx", "gy"),
            P("gx", "gy"),
            P("gx", "gy"),
            P(("gx", "gy"), None),
            P(("gx", "gy"), None),
            P(),
        ),
        out_specs=(P("tracer", None, "gx", "gy"), P("tracer", ("gx", "gy"))),
        check_vma=False,
    )
```

time: 2230 us -> 86.3 us (0.04)
  waiting for transfers between devices: 1550 us -> 13.6 us
  local copies, waits for them, and re-layouts: 364 us -> 3.39 us
  blocking collectives: 176 us -> 0 us
  other arithmetic: 84.2 us -> 0.15 us
  Pallas kernels: 0 us -> 31.2 us
  starting transfers between devices: 9.53 us -> 35.8 us
    unnamed x3 -> x0, waiting for transfers between devices: 1530 us -> none
    gather x5 -> x0, local copies, waits for them, and re-layouts: 280 us -> none  [the longest x2 273 us: profile(): chosen = jnp.take_along_axis(prof, jnp.clip(offset, 0, FP - 1), axis=1)]
    all_gather x1 -> x0, blocking collectives: 176 us -> none  [per_device(): lax.all_gather((footprint, corners), ('gx', 'gy'), axis=0, tiled=True)]
    concatenate x3 -> x0, other arithmetic: 42.3 us -> none  [padded_2(): jnp.concatenate([lax.ppermute(tail, axis, [(i, (i + 1) % count) for i in...]
    pallas_call x0 -> x4, Pallas kernels: none -> 31.2 us  [the longest x1 14.2 us: advance(): pl.pallas_call(functools.partial(step_kernel, nz), grid=(nz,), in_specs=[...]
    slice x6 -> x1, local copies, waits for them, and re-layouts: 27.4 us -> 0.52 us  [one_round(): return (jnp.sum(parts, axis=0), most[0, 0])]
    unnamed x54 -> x16, local copies, waits for them, and re-layouts: 28.1 us -> 2.87 us
    all_to_all x0 -> x2, starting transfers between devices: none -> 25.1 us  [the longest x1 13.6 us: one_round(): parts = lax.all_to_all(parts, TILES, 0, 0)]
  transfers between devices with their start and end apart: 6 -> 6, of which waited for: 2 -> 3; matrix products, arithmetic and copies ran while one was open for 6% -> 1% of each run, Pallas kernels for 0% -> 24%
where the time goes in v1:
time: 86.3 us; the launch traced here: 85.5 us
  starting transfers between devices  35.8 us (41%)
  Pallas kernels  31.2 us (36%)
  waiting for transfers between devices  13.6 us (16%)
  local copies, waits for them, and re-layouts  3.39 us (4%)
  between operations  1.4 us (2%)
    pallas_call x1, Pallas kernels, advance(): pl.pallas_call(functools.partial(step_kernel, nz), grid=(nz,), in_specs=[...  14.2 us
    all_to_all x1, starting transfers between devices, one_round(): parts = lax.all_to_all(parts, TILES, 0, 0)  13.6 us
    all_to_all x1, starting transfers between devices, one_round(): rows = lax.all_to_all(sent.reshape(tiles, CAP, LANES), TILES, 0, 0)  11.5 us
    pallas_call x1, Pallas kernels, observe(): pl.pallas_call(functools.partial(observe_kernel, nz, sources), in_specs=[...  8.75 us
    all_to_all x1, waiting for transfers between devices, one_round(): parts = lax.all_to_all(parts, TILES, 0, 0)  8.62 us
    pallas_call x1, Pallas kernels, edges(): pl.pallas_call(functools.partial(edges_kernel, nz), grid=(nz // zb,), in_...  6.13 us
    ppermute x1, starting transfers between devices, per_device(): lax.ppermute(east, 'gx', up_x)  4.55 us
    ppermute x1, waiting for transfers between devices, per_device(): lax.ppermute(south, 'gy', [(b, a) for a, b in up_y])  4.17 us
  transfers between devices with their start and end apart: 6, of which 3 were waited for; matrix products, arithmetic and copies ran while one was open for 1% of the time, Pallas kernels for 24%

profile of v1, /device:TPU:0, one launch (start us, length us, event | category | flops | bytes accessed | tf_op | source)
XLA Modules:
  0.0 85.5 jit_solution(96159708615111046)
XLA Ops:
  0.6 0.9 %copy.12.fp_ref = f32[128,80]{1,0:T(8,128)S(1)} copy(f32[128,80]{0,1:T(8,128)} %param.17) | data formatting | bytes 81920 | tf_op args[6]
  1.5 0.8 copy.13.corner_ref
  2.3 2.1 %pack.2 = f32[1536,128]{1,0:T(8,128)} custom-call(s32[1]{0:T(128)} %constant.39.clone.1.round_ref, f32[128,80]{1,0:T(8,128)S(1)} %copy.12.fp_ref, s32[128,2]{1,0:T(8,128)S(1)} %copy.13.corner_ref, s32[2,128]{1,0:T(2,128)} %bitcast.23), custom_call_target="tpu_custom_call" | custom-call | tf_op jit(solution)/shard_map/pack/pallas_call | solution.py:235
  4.4 11.5 %all-to-all-start.2 = ((f32[64,24,128]{2,1,0:T(8,128)}), f32[64,24,128]{2,1,0:T(8,128)S(1)}, u32[]{:S(2)}, u32[]{:S(2)}) async-start(f32[64,24,128]{2,1,0:T(8,128)} %bitcast.8), calls=%async_computation.2 | async-start | bytes 1572864 | tf_op jit(solution)/shard_map/all_to_all | solution.py:330
  15.9 6.1 %edges.1 = (f32[96,128]{1,0:T(8,128)}, f32[80,128]{1,0:T(8,128)}, f32[128,128]{1,0:T(8,128)}, f32[128,128]{1,0:T(8,128)}) custom-call(f32[4,16,128,128]{3,2,1,0:T(8,128)} %c_ref.3, f32[16,128,128]{2,1,0:T(8,128)} %we_ref.3, f32[16,128,128]{2,1,0:T(8,128)} %wn_ref.3, f32[16,128,128]{2,1,0:T(8,128)} %k_ref.3), custom_call_target="tpu_custom_call" | custom-call | tf_op jit(solution)/shard_map/edges/pallas_call | solution.py:59
  22.0 0.0 copy-start.6
  22.0 1.4 %collective-permute-start.1 = (f32[80,128]{1,0:T(8,128)}, f32[80,128]{1,0:T(8,128)S(1)}, u32[]{:S(2)}, u32[]{:S(2)}) collective-permute-start(f32[80,128]{1,0:T(8,128)} %get-tuple-element.55), channel_id=1, source_target_pairs={{8,0},{16,8},{24,16},{32,24},{40,32},{48,40},{56,48},{9,1},{17,9},... | collective-permute-start | bytes 122888 | tf_op jit(solution)/shard_map/ppermute | solution.py:314
  23.4 4.5 %collective-permute-start = (f32[96,128]{1,0:T(8,128)}, f32[96,128]{1,0:T(8,128)S(1)}, u32[]{:S(2)}, u32[]{:S(2)}) collective-permute-start(f32[96,128]{1,0:T(8,128)} %get-tuple-element.54), channel_id=1, source_target_pairs={{0,8},{8,16},{16,24},{24,32},{32,40},{40,48},{48,56},{1,9},{9,17},... | collective-permute-start | bytes 147464 | tf_op jit(solution)/shard_map/ppermute | solution.py:313
  28.0 3.5 %collective-permute-start.2 = (f32[128,128]{1,0:T(8,128)}, f32[128,128]{1,0:T(8,128)S(1)}, u32[]{:S(2)}, u32[]{:S(2)}) collective-permute-start(f32[128,128]{1,0:T(8,128)} %get-tuple-element.56), channel_id=1, source_target_pairs={{0,1},{1,2},{2,3},{3,4},{4,5},{5,6},{6,7},{8,9},{9,10},{10,11},{11... | collective-permute-start | bytes 196616 | tf_op jit(solution)/shard_map/ppermute | solution.py:315
  31.5 1.3 %collective-permute-start.3 = (f32[128,128]{1,0:T(8,128)}, f32[128,128]{1,0:T(8,128)S(1)}, u32[]{:S(2)}, u32[]{:S(2)}) collective-permute-start(f32[128,128]{1,0:T(8,128)} %get-tuple-element.57), channel_id=1, source_target_pairs={{1,0},{2,1},{3,2},{4,3},{5,4},{6,5},{7,6},{9,8},{10,9},{11,10},{12... | collective-permute-start | bytes 196616 | tf_op jit(solution)/shard_map/ppermute | solution.py:316
  32.8 0.1 pad_add_fusion.origin_ref
  32.9 0.0 collective-permute-done.1.he_ref
  32.9 0.0 copy-start.5
  32.9 0.0 collective-permute-done.hw_ref
  32.9 0.0 copy-start.4
  32.9 0.8 collective-permute-done.2.hs_ref
  33.7 0.0 copy-start.2
  33.7 4.2 %collective-permute-done.3.hn_ref = f32[128,128]{1,0:T(8,128)S(1)} collective-permute-done((f32[128,128]{1,0:T(8,128)}, f32[128,128]{1,0:T(8,128)S(1)}, u32[]{:S(2)}, u32[]{:S(2)}) %collective-permute-start.3) | collective-permute-done | bytes 65568 | tf_op jit(solution)/shard_map/ppermute | solution.py:316
  37.8 0.0 copy-start.3
  37.8 0.0 copy-done.5
  37.8 0.0 copy-done.4
  37.9 0.0 copy-done.2
  37.9 0.6 copy-done.3
  38.5 0.0 copy-start
  38.5 14.2 %advance.1 = (f32[4,16,128,128]{3,2,1,0:T(8,128)}, bf16[2048,512]{1,0:T(8,128)(2,1)S(1)}) custom-call(s32[1]{0:T(128)} %bitcast.4.first_ref, f32[4,16,128,128]{3,2,1,0:T(8,128)} %c_ref.3, f32[16,128,128]{2,1,0:T(8,128)} %we_ref.3, f32[16,128,128]{2,1,0:T(8,128)} %wn_ref.3, f32[16,128,128]{2,1,0:T(8,128)} %k_ref.3, f32[128,128]{1,0:T(8,128)} %em_ref.1, ...), custom_call_target="tpu_custom_call" | custom-call | flops 41943040 | bytes 13631488 | tf_op jit(solution)/shard_map/advance/pallas_call | solution.py:153
  52.7 0.0 all-to-all-done.2
  52.7 0.0 copy-done.6
  52.7 8.8 %observe.2 = (f32[64,4,128]{2,1,0:T(4,128)}, s32[8,128]{1,0:T(8,128)S(1)}) custom-call(s32[2]{0:T(128)S(1)} %pad_add_fusion.origin_ref, s32[64]{0:T(128)S(1)} %copy-done.6, f32[1536,128]{1,0:T(8,128)S(1)} %bitcast.22, bf16[2048,512]{1,0:T(8,128)(2,1)S(1)} %get-tuple-element.146.r_ref), custom_call_target="tpu_custom_call" | custom-call | tf_op jit(solution)/shard_map/observe/pallas_call | solution.py:287
  61.4 13.6 %all-to-all-start.3 = ((f32[64,4,128]{2,1,0:T(4,128)}), f32[64,4,128]{2,1,0:T(4,128)S(1)}, u32[]{:S(2)}, u32[]{:S(2)}) async-start(f32[64,4,128]{2,1,0:T(4,128)} %get-tuple-element.60), calls=%async_computation.3 | async-start | bytes 262144 | tf_op jit(solution)/shard_map/all_to_all | solution.py:334
  75.0 0.5 slice.3
  76.2 8.6 %all-to-all-done.3 = f32[64,4,128]{2,1,0:T(4,128)S(1)} async-done(((f32[64,4,128]{2,1,0:T(4,128)}), f32[64,4,128]{2,1,0:T(4,128)S(1)}, u32[]{:S(2)}, u32[]{:S(2)}) %all-to-all-start.3) | async-done | bytes 131104 | tf_op jit(solution)/shard_map/all_to_all | solution.py:334
  84.8 0.1 reduce_sum.18
  84.9 0.0 copy-done
  84.9 0.0 copy-start.1
  84.9 0.6 copy-done.1
  (1 shorter events, 0.0 us)
Async XLA Ops:
  4.4 48.3 %all-to-all-start.2 = ((f32[64,24,128]{2,1,0:T(8,128)}), f32[64,24,128]{2,1,0:T(8,128)S(1)}, u32[]{:S(2)}, u32[]{:S(2)}) async-start(f32[64,24,128]{2,1,0:T(8,128)} %bitcast.8), calls=%async_computation.2 | async-start | bytes 1572864 | tf_op jit(solution)/shard_map/all_to_all | solution.py:330
  22.0 30.7 %copy-start.6 = (s32[64]{0:T(128)S(1)}, s32[64]{0:T(128)}, u32[]{:S(2)}) copy-start(s32[64]{0:T(128)} %owner_ref.1) | copy-start | bytes 772
  22.0 10.8 %collective-permute-start.1 = (f32[80,128]{1,0:T(8,128)}, f32[80,128]{1,0:T(8,128)S(1)}, u32[]{:S(2)}, u32[]{:S(2)}) collective-permute-start(f32[80,128]{1,0:T(8,128)} %get-tuple-element.55), channel_id=1, source_target_pairs={{8,0},{16,8},{24,16},{32,24},{40,32},{48,40},{56,48},{9,1},{17,9},... | collective-permute-start | bytes 122888 | tf_op jit(solution)/shard_map/ppermute | solution.py:314
  23.4 9.4 %collective-permute-start = (f32[96,128]{1,0:T(8,128)}, f32[96,128]{1,0:T(8,128)S(1)}, u32[]{:S(2)}, u32[]{:S(2)}) collective-permute-start(f32[96,128]{1,0:T(8,128)} %get-tuple-element.54), channel_id=1, source_target_pairs={{0,8},{8,16},{16,24},{24,32},{32,40},{40,48},{48,56},{1,9},{9,17},... | collective-permute-start | bytes 147464 | tf_op jit(solution)/shard_map/ppermute | solution.py:313
  28.0 5.7 %collective-permute-start.2 = (f32[128,128]{1,0:T(8,128)}, f32[128,128]{1,0:T(8,128)S(1)}, u32[]{:S(2)}, u32[]{:S(2)}) collective-permute-start(f32[128,128]{1,0:T(8,128)} %get-tuple-element.56), channel_id=1, source_target_pairs={{0,1},{1,2},{2,3},{3,4},{4,5},{5,6},{6,7},{8,9},{9,10},{10,11},{11... | collective-permute-start | bytes 196616 | tf_op jit(solution)/shard_map/ppermute | solution.py:315
  31.5 6.4 %collective-permute-start.3 = (f32[128,128]{1,0:T(8,128)}, f32[128,128]{1,0:T(8,128)S(1)}, u32[]{:S(2)}, u32[]{:S(2)}) collective-permute-start(f32[128,128]{1,0:T(8,128)} %get-tuple-element.57), channel_id=1, source_target_pairs={{1,0},{2,1},{3,2},{4,3},{5,4},{6,5},{7,6},{9,8},{10,9},{11,10},{12... | collective-permute-start | bytes 196616 | tf_op jit(solution)/shard_map/ppermute | solution.py:316
  32.9 5.0 %copy-start.5 = (f32[80,128]{1,0:T(8,128)}, f32[80,128]{1,0:T(8,128)S(1)}, u32[]{:S(2)}) copy-start(f32[80,128]{1,0:T(8,128)S(1)} %collective-permute-done.1.he_ref) | copy-start | bytes 122884
  32.9 5.0 %copy-start.4 = (f32[96,128]{1,0:T(8,128)}, f32[96,128]{1,0:T(8,128)S(1)}, u32[]{:S(2)}) copy-start(f32[96,128]{1,0:T(8,128)S(1)} %collective-permute-done.hw_ref) | copy-start | bytes 147460
  33.7 4.2 %copy-start.2 = (f32[128,128]{1,0:T(8,128)}, f32[128,128]{1,0:T(8,128)S(1)}, u32[]{:S(2)}) copy-start(f32[128,128]{1,0:T(8,128)S(1)} %collective-permute-done.2.hs_ref) | copy-start | bytes 196612
  37.8 0.6 copy-start.3
  38.5 46.4 %copy-start = (s32[128,2]{0,1:T(2,128)S(1)}, s32[128,2]{0,1:T(2,128)}, u32[]{:S(2)}) copy-start(s32[128,2]{0,1:T(2,128)} %param.18) | copy-start | bytes 3076
  61.4 23.4 %all-to-all-start.3 = ((f32[64,4,128]{2,1,0:T(4,128)}), f32[64,4,128]{2,1,0:T(4,128)S(1)}, u32[]{:S(2)}, u32[]{:S(2)}) async-start(f32[64,4,128]{2,1,0:T(4,128)} %get-tuple-element.60), calls=%async_computation.3 | async-start | bytes 262144 | tf_op jit(solution)/shard_map/all_to_all | solution.py:334
  84.9 0.6 copy-start.1

commit v2 on v1

v2 whole, which is shorter than its diff:
```python
import functools
import math

import jax
import jax.numpy as jnp
from jax import lax
from jax.experimental import pallas as pl
from jax.experimental.pallas import tpu as pltpu
from jax.sharding import PartitionSpec as P

FP = 32
CAP = 24
LANES = 128
TILES = ("gx", "gy")


def edges_kernel(
    nz, c_ref, we_ref, wn_ref, k_ref, e_ref, w_ref, n_ref, s_ref, ct_ref, wnt_ref, kt_ref
):
    count, zb = c_ref.shape[0], c_ref.shape[1]
    cols_x, cols_y = c_ref.shape[2], c_ref.shape[3]
    step = pl.program_id(0)

    def ends(slot, cells, flipped):
        e_ref[pl.ds(slot, 1), :] = cells[cols_x - 1 : cols_x, :]
        w_ref[pl.ds(slot, 1), :] = cells[0:1, :]
        n_ref[pl.ds(slot, 1), :] = flipped[cols_y - 1 : cols_y, :]
        s_ref[pl.ds(slot, 1), :] = flipped[0:1, :]

    for zi in range(zb):
        z = step * zb + zi
        for t in range(count):
            cells = c_ref[t, zi]
            flipped = cells.T
            ct_ref[t, zi] = flipped
            ends(t * nz + z, cells, flipped)
        cells = k_ref[zi]
        flipped = cells.T
        kt_ref[zi] = flipped
        ends(count * nz + z, cells, flipped)
        slot = (count + 1) * nz + z
        flipped = wn_ref[zi].T
        wnt_ref[zi] = flipped
        e_ref[pl.ds(slot, 1), :] = we_ref[zi, cols_x - 1 : cols_x, :]
        n_ref[pl.ds(slot, 1), :] = flipped[cols_y - 1 : cols_y, :]


def edges(tracers, wind_east, wind_north, diffusivity):
    count, nz, cols_x, cols_y = tracers.shape
    zb = 4
    f32 = jnp.float32
    level = pl.BlockSpec((zb, cols_x, cols_y), lambda i: (i, 0, 0))
    fields = pl.BlockSpec((count, zb, cols_x, cols_y), lambda i: (0, i, 0, 0))
    flat = [(count + 2, cols_y), (count + 1, cols_y), (count + 2, cols_x), (count + 1, cols_x)]
    return pl.pallas_call(
        functools.partial(edges_kernel, nz),
        grid=(nz // zb,),
        in_specs=[fields, level, level, level],
        out_specs=[
            *[pl.BlockSpec((n * nz, width), lambda i: (0, 0)) for n, width in flat],
            pl.BlockSpec((count, zb, cols_y, cols_x), lambda i: (0, i, 0, 0)),
            pl.BlockSpec((zb, cols_y, cols_x), lambda i: (i, 0, 0)),
            pl.BlockSpec((zb, cols_y, cols_x), lambda i: (i, 0, 0)),
        ],
        out_shape=[
            *[jax.ShapeDtypeStruct((n * nz, width), f32) for n, width in flat],
            jax.ShapeDtypeStruct((count, nz, cols_y, cols_x), f32),
            jax.ShapeDtypeStruct((nz, cols_y, cols_x), f32),
            jax.ShapeDtypeStruct((nz, cols_y, cols_x), f32),
        ],
        compiler_params=pltpu.CompilerParams(vmem_limit_bytes=24 << 20),
        name="edges",
    )(tracers, wind_east, wind_north, diffusivity)


def step_kernel(
    nz, first_ref, c_ref, ct_ref, we_ref, wnt_ref, k_ref, kt_ref, em_ref, tag_ref,
    hw_ref, he_ref, hs_ref, hn_ref, out_ref, r_ref,
):
    count, zb = c_ref.shape[0], c_ref.shape[1]
    cols_x, cols_y = c_ref.shape[2], c_ref.shape[3]
    step = pl.program_id(0)

    def before(a, halo_ref, slot):
        row = lax.broadcasted_iota(jnp.int32, a.shape, 0)
        return jnp.where(row == 0, halo_ref[pl.ds(slot, 1), :], pltpu.roll(a, 1, 0))

    def after(a, halo_ref, slot):
        last = a.shape[0] - 1
        row = lax.broadcasted_iota(jnp.int32, a.shape, 0)
        return jnp.where(row == last, halo_ref[pl.ds(slot, 1), :], pltpu.roll(a, last, 0))

    def coefficients(wind, k, low_ref, high_ref, z):
        at_k, at_w = count * nz + z, (count + 1) * nz + z
        mix = 0.5 * (k + after(k, high_ref, at_k))
        mix_m = 0.5 * (k + before(k, low_ref, at_k))
        wind_m = before(wind, low_ref, at_w)
        own = jnp.maximum(wind, 0.0) + mix - (jnp.minimum(wind_m, 0.0) - mix_m)
        return own, mix - jnp.minimum(wind, 0.0), jnp.maximum(wind_m, 0.0) + mix_m

    for zi in range(zb):
        z = step * zb + zi
        own_x, next_x, prev_x = coefficients(we_ref[zi], k_ref[zi], hw_ref, he_ref, z)
        own_y, next_y, prev_y = coefficients(wnt_ref[zi], kt_ref[zi], hs_ref, hn_ref, z)
        own_x = 1.0 - own_x
        for t in range(count):
            slot = t * nz + z
            ct = ct_ref[t, zi]
            part_y = (
                next_y * after(ct, hn_ref, slot) + prev_y * before(ct, hs_ref, slot) - own_y * ct
            )
            c = c_ref[t, zi]
            part_x = (
                own_x * c + next_x * after(c, he_ref, slot) + prev_x * before(c, hw_ref, slot)
            )
            new = part_x + part_y.T
            if zi == 0:
                hit = (tag_ref[...] == first_ref[0] + t) & (step == 0)
                new = new + jnp.where(hit, em_ref[...], 0.0)
            out_ref[t, zi] = new
            r_ref[t * cols_y : (t + 1) * cols_y, zi * cols_x : (zi + 1) * cols_x] = new.T.astype(
                jnp.bfloat16
            )


def advance(first, tracers, tracers_t, wind_east, wind_north_t, k, k_t, emission, tag, halos):
    count, nz, cols_x, cols_y = tracers.shape
    zb = 2
    level = pl.BlockSpec((zb, cols_x, cols_y), lambda i: (i, 0, 0))
    level_t = pl.BlockSpec((zb, cols_y, cols_x), lambda i: (i, 0, 0))

    def whole(a):
        return pl.BlockSpec(a.shape, lambda i: (0, 0))

    fields = pl.BlockSpec((count, zb, cols_x, cols_y), lambda i: (0, i, 0, 0))
    fields_t = pl.BlockSpec((count, zb, cols_y, cols_x), lambda i: (0, i, 0, 0))
    return pl.pallas_call(
        functools.partial(step_kernel, nz),
        grid=(nz // zb,),
        in_specs=[
            pl.BlockSpec(memory_space=pltpu.SMEM),
            fields,
            fields_t,
            level,
            level_t,
            level,
            level_t,
            whole(emission),
            whole(tag),
            *[whole(h) for h in halos],
        ],
        out_specs=[fields, pl.BlockSpec((count * cols_y, zb * cols_x), lambda i: (0, i))],
        out_shape=[
            jax.ShapeDtypeStruct(tracers.shape, jnp.float32),
            jax.ShapeDtypeStruct((count * cols_y, nz * cols_x), jnp.bfloat16),
        ],
        cost_estimate=pl.CostEstimate(
            flops=40 * tracers.size, bytes_accessed=18 << 20, transcendentals=0
        ),
        compiler_params=pltpu.CompilerParams(vmem_limit_bytes=24 << 20),
        name="advance",
    )(first, tracers, tracers_t, wind_east, wind_north_t, k, k_t, emission, tag, *halos)


def pack_kernel(
    tiles_x, tiles_y, size, nz, number_ref, owner_ref, fp_ref, corner_ref, out_ref, m_ref
):
    tiles = tiles_x * tiles_y
    obs = fp_ref.shape[1]
    width = 2 * FP + nz
    tile = lax.broadcasted_iota(jnp.int32, (tiles, obs), 0)
    first_x = (tile // tiles_y) * size[0]
    first_y = (tile % tiles_y) * size[1]
    x0 = corner_ref[0:1, :]
    y0 = corner_ref[1:2, :]
    touch = (
        (x0 < first_x + size[0])
        & (x0 + FP > first_x)
        & (y0 < first_y + size[1])
        & (y0 + FP > first_y)
    )
    ones = jnp.where(touch, 1.0, 0.0)
    earlier = lax.broadcasted_iota(jnp.int32, (obs, obs), 0) < lax.broadcasted_iota(
        jnp.int32, (obs, obs), 1
    )
    rank = jnp.dot(
        ones.astype(jnp.bfloat16),
        jnp.where(earlier, 1.0, 0.0).astype(jnp.bfloat16),
        preferred_element_type=jnp.float32,
    ).astype(jnp.int32)
    most = jnp.max(jnp.sum(ones, axis=1, keepdims=True), axis=0, keepdims=True)
    slot = jnp.where(touch, rank - number_ref[0] * CAP, -1)
    which = lax.broadcasted_iota(jnp.int32, (tiles, CAP, obs), 1)
    pick = jnp.where(slot[:, None, :] == which, 1.0, 0.0).reshape(tiles * CAP, obs)
    pick = pick.astype(jnp.bfloat16)

    def rotated(profile, by):
        shift = 1
        while shift < FP:
            turn = (by & shift) != 0
            profile = jnp.where(turn, pltpu.roll(profile, shift, 0), profile)
            shift *= 2
        return profile

    m_ref[0:FP, :] = rotated(fp_ref[0:FP, :], x0)
    m_ref[FP : 2 * FP, :] = rotated(fp_ref[FP : 2 * FP, :], y0)
    m_ref[2 * FP : width, :] = fp_ref[2 * FP : width, :]
    m_ref[width:, :] = jnp.zeros_like(m_ref[width:, :])
    m_ref[width : width + 2, :] = corner_ref[...].astype(jnp.float32)
    m_ref[width + 2 : width + 3, :] = lax.broadcasted_iota(jnp.int32, (1, obs), 1).astype(
        jnp.float32
    )
    rows = m_ref[...].T
    lane = lax.broadcasted_iota(jnp.int32, rows.shape, 1)
    high = rows.astype(jnp.bfloat16)
    low = jnp.where(lane < 2 * FP, 0.0, rows - high.astype(jnp.float32)).astype(jnp.bfloat16)
    packed = jnp.dot(pick, high, preferred_element_type=jnp.float32) + jnp.dot(
        pick, low, preferred_element_type=jnp.float32
    )
    lane = lax.broadcasted_iota(jnp.int32, packed.shape, 1)
    packed = jnp.where(lane == width + 3, most, packed)
    owner = owner_ref[number_ref[1]].astype(jnp.float32)
    out_ref[...] = jnp.where(lane == width + 4, owner, packed)


def pack(number, owner_map, footprint, corners, tiles_x, tiles_y, size):
    obs, width = footprint.shape
    nz = width - 2 * FP
    tiles = tiles_x * tiles_y
    vmem = pl.BlockSpec(memory_space=pltpu.VMEM)
    smem = pl.BlockSpec(memory_space=pltpu.SMEM)
    return pl.pallas_call(
        functools.partial(pack_kernel, tiles_x, tiles_y, size, nz),
        in_specs=[smem, smem, vmem, vmem],
        out_specs=vmem,
        out_shape=jax.ShapeDtypeStruct((tiles * CAP, LANES), jnp.float32),
        scratch_shapes=[pltpu.VMEM((LANES, obs), jnp.float32)],
        compiler_params=pltpu.CompilerParams(vmem_limit_bytes=24 << 20),
        name="pack",
    )(number, owner_map, footprint.T, corners.T)


def observe_kernel(nz, count, origin_ref, rows_ref, r_ref, out_ref, most_ref, w_ref):
    cols = LANES
    chunk = w_ref.shape[1]
    scale = 1.0 / (FP * math.sqrt(nz))
    width = 2 * FP + nz
    out_ref[...] = jnp.zeros_like(out_ref)

    def body(step, most):
        rows = rows_ref[pl.ds(pl.multiple_of(step * chunk, chunk), chunk), :].T
        place = lax.broadcasted_iota(jnp.int32, (cols, chunk), 0)

        def along(profile, corner, origin):
            offset = place - (corner.astype(jnp.int32) - origin)
            inside = (offset >= 0) & (offset < FP)
            return jnp.where(inside, jnp.concatenate([profile] * (cols // FP), axis=0), 0.0)

        wx = along(rows[0:FP], rows[width : width + 1], origin_ref[0])
        for z in range(nz):
            part = wx * rows[2 * FP + z : 2 * FP + z + 1]
            w_ref[z * cols : (z + 1) * cols, :] = part.astype(jnp.bfloat16)
        got = jnp.dot(r_ref[...], w_ref[...], preferred_element_type=jnp.float32)
        wy = along(rows[FP : 2 * FP], rows[width + 1 : width + 2], origin_ref[1]) * scale
        values = [
            jnp.sum(got[t * cols : (t + 1) * cols] * wy, axis=0, keepdims=True)
            for t in range(count)
        ]
        values = jnp.concatenate(values * (8 // count), axis=0)
        lines = out_ref.shape[0]
        owner = lax.broadcasted_iota(jnp.int32, (lines, chunk), 0) // count
        mine = owner == rows[width + 4 : width + 5].astype(jnp.int32)
        spread = jnp.where(mine, jnp.concatenate([values] * (lines // 8), axis=0), 0.0)
        high = spread.astype(jnp.bfloat16)
        low = (spread - high.astype(jnp.float32)).astype(jnp.bfloat16)
        obs = jnp.where(place == rows[width + 2 : width + 3].astype(jnp.int32), 1.0, 0.0)
        obs = obs.astype(jnp.bfloat16)
        across = (((1,), (1,)), ((), ()))
        out_ref[...] += lax.dot_general(
            high, obs, across, preferred_element_type=jnp.float32
        ) + lax.dot_general(low, obs, across, preferred_element_type=jnp.float32)
        return jnp.maximum(most, jnp.max(rows[width + 3 : width + 4], axis=1, keepdims=True))

    chunks = rows_ref.shape[0] // chunk
    most = lax.fori_loop(0, chunks, body, jnp.zeros((1, 1), jnp.float32))
    most_ref[...] = jnp.broadcast_to(most, most_ref.shape).astype(jnp.int32)


def observe(origin, rows, rounded, count, nz, sources):
    vmem = pl.BlockSpec(memory_space=pltpu.VMEM)
    smem = pl.BlockSpec(memory_space=pltpu.SMEM)
    return pl.pallas_call(
        functools.partial(observe_kernel, nz, count),
        in_specs=[smem, vmem, vmem],
        out_specs=[vmem, vmem],
        out_shape=[
            jax.ShapeDtypeStruct((sources * count, LANES), jnp.float32),
            jax.ShapeDtypeStruct((8, LANES), jnp.int32),
        ],
        scratch_shapes=[pltpu.VMEM((rounded.shape[1], 512), jnp.bfloat16)],
        compiler_params=pltpu.CompilerParams(vmem_limit_bytes=24 << 20),
        name="observe",
    )(origin, rows, rounded)


def per_device(
    tracers, wind_east, wind_north, diffusivity, emission, region_tag, footprint, corners, owner_map
):
    count, nz, cols_x, cols_y = tracers.shape
    tiles_x, tiles_y = lax.axis_size("gx"), lax.axis_size("gy")
    tiles = tiles_x * tiles_y
    obs = footprint.shape[0]

    east, west, north, south, tracers_t, wind_north_t, k_t = edges(
        tracers, wind_east, wind_north, diffusivity
    )
    up_x = [(i, i + 1) for i in range(tiles_x - 1)]
    up_y = [(i, i + 1) for i in range(tiles_y - 1)]
    halos = (
        lax.ppermute(east, "gx", up_x),
        lax.ppermute(west, "gx", [(b, a) for a, b in up_x]),
        lax.ppermute(north, "gy", up_y),
        lax.ppermute(south, "gy", [(b, a) for a, b in up_y]),
    )
    first = (lax.axis_index("tracer") * count).astype(jnp.int32).reshape(1)
    stepped, rounded = advance(
        first, tracers, tracers_t, wind_east, wind_north_t, diffusivity, k_t,
        emission, region_tag, halos,
    )
    origin = jnp.stack([lax.axis_index("gx") * cols_x, lax.axis_index("gy") * cols_y])
    origin = origin.astype(jnp.int32)
    me = lax.axis_index(TILES).astype(jnp.int32)

    def one_round(number):
        sent = pack(
            jnp.stack([number, me]), owner_map, footprint, corners, tiles_x, tiles_y, (cols_x, cols_y),
        )
        rows = lax.all_to_all(sent.reshape(tiles, CAP, LANES), TILES, 0, 0)
        parts, most = observe(
            origin, rows.reshape(tiles * CAP, LANES), rounded, count, nz, tiles
        )
        parts = lax.all_to_all(parts.reshape(tiles, count, obs), TILES, 0, 0)
        return jnp.sum(parts, axis=0), most[0, 0]

    observed, most = one_round(jnp.int32(0))
    rounds = (most + CAP - 1) // CAP
    observed = lax.fori_loop(
        jnp.int32(1), rounds, lambda r, total: total + one_round(r)[0], observed
    )
    return (stepped, observed)


def solution(mesh):
    return jax.shard_map(
        per_device,
        mesh=mesh,
        in_specs=(
            P("tracer", None, "gx", "gy"),
            P(None, "gx", "gy"),
            P(None, "gx", "gy"),
            P(None, "gx", "gy"),
            P("gx", "gy"),
            P("gx", "gy"),
            P(("gx", "gy"), None),
            P(("gx", "gy"), None),
            P(),
        ),
        out_specs=(P("tracer", None, "gx", "gy"), P("tracer", ("gx", "gy"))),
        check_vma=False,
    )
```

time: 86.3 us -> 88.1 us (1.021)
  local copies, waits for them, and re-layouts: 3.39 us -> 17.8 us
  Pallas kernels: 31.2 us -> 19.2 us
    unnamed x16 -> x38, local copies, waits for them, and re-layouts: 2.87 us -> 17.2 us
    pallas_call x2, Pallas kernels: 23 us -> 14.7 us  [the longest x1 7.42 us: advance(): pl.pallas_call(functools.partial(step_kernel, nz), grid=(nz // zb,), in_s...]
    pallas_call x1, Pallas kernels: 6.13 us -> 2.31 us  [edges(): pl.pallas_call(functools.partial(edges_kernel, nz), grid=(nz // zb,), in_...]
    ppermute x1, waiting for transfers between devices: 0.01 us -> 3.21 us  [per_device(): lax.ppermute(west, 'gx', [(b, a) for a, b in up_x])]
    ppermute x1, waiting for transfers between devices: 4.17 us -> 1.3 us  [per_device(): lax.ppermute(south, 'gy', [(b, a) for a, b in up_y])]
    ppermute x1, starting transfers between devices: 4.55 us -> 3.47 us  [per_device(): lax.ppermute(east, 'gx', up_x)]
  transfers between devices with their start and end apart: 6 -> 6, of which waited for: 3 -> 3; matrix products, arithmetic and copies ran while one was open for 1% -> 1% of each run, Pallas kernels for 24% -> 11%
where the time goes in v2:
time: 88.1 us; the launch traced here: 87.3 us
  starting transfers between devices  35.5 us (40%)
  Pallas kernels  19.2 us (22%)
  local copies, waits for them, and re-layouts  17.8 us (20%)
  waiting for transfers between devices  13 us (15%)
  between operations  1.52 us (2%)
    unnamed x38, local copies, waits for them, and re-layouts  17.2 us
    all_to_all x1, starting transfers between devices, one_round(): parts = lax.all_to_all(parts.reshape(tiles, count, obs), TILES, 0, 0)  14.4 us
    all_to_all x1, starting transfers between devices, one_round(): rows = lax.all_to_all(sent.reshape(tiles, CAP, LANES), TILES, 0, 0)  11.6 us
    all_to_all x1, waiting for transfers between devices, one_round(): parts = lax.all_to_all(parts.reshape(tiles, count, obs), TILES, 0, 0)  8.49 us
    pallas_call x1, Pallas kernels, advance(): pl.pallas_call(functools.partial(step_kernel, nz), grid=(nz // zb,), in_s...  7.42 us
    pallas_call x1, Pallas kernels, observe(): pl.pallas_call(functools.partial(observe_kernel, nz, count), in_specs=[sm...  7.3 us
    ppermute x1, starting transfers between devices, per_device(): lax.ppermute(east, 'gx', up_x)  3.47 us
    ppermute x1, starting transfers between devices, per_device(): lax.ppermute(north, 'gy', up_y)  3.37 us
  transfers between devices with their start and end apart: 6, of which 3 were waited for; matrix products, arithmetic and copies ran while one was open for 1% of the time, Pallas kernels for 11%

profile of v2, /device:TPU:0, one launch (start us, length us, event | category | flops | bytes accessed | tf_op | source)
XLA Modules:
  0.0 87.3 jit_solution(4946000558777338498)
XLA Ops:
  0.6 0.1 pad_add_fusion.2.number_ref
  0.7 2.2 %pack.2 = f32[1536,128]{1,0:T(8,128)} custom-call(s32[2]{0:T(128)S(1)} %pad_add_fusion.2.number_ref, s32[64]{0:T(128)} %owner_ref.1, f32[80,128]{1,0:T(8,128)} %bitcast.35, s32[2,128]{1,0:T(2,128)} %bitcast.37), custom_call_target="tpu_custom_call" | custom-call | tf_op jit(solution)/shard_map/pack/pallas_call | solution.py:232
  2.9 0.0 copy-start.13
  2.9 0.0 copy-start.14
  2.9 11.6 %all-to-all-start.2 = ((f32[64,24,128]{2,1,0:T(8,128)}), f32[64,24,128]{2,1,0:T(8,128)S(1)}, u32[]{:S(2)}, u32[]{:S(2)}) async-start(f32[64,24,128]{2,1,0:T(8,128)} %bitcast.13), calls=%async_computation.2 | async-start | bytes 1572864 | tf_op jit(solution)/shard_map/all_to_all | solution.py:338
  14.5 0.0 copy-start
  14.6 2.2 %copy-done = f32[4,16,128,128]{3,2,1,0:T(8,128)S(1)} copy-done((f32[4,16,128,128]{3,2,1,0:T(8,128)S(1)}, f32[4,16,128,128]{3,2,1,0:T(8,128)}, u32[]{:S(2)}) %copy-start) | copy-done | bytes 4194328
  16.7 0.0 copy-start.4
  16.7 1.2 %copy-done.4 = f32[16,128,128]{2,1,0:T(8,128)S(1)} copy-done((f32[16,128,128]{2,1,0:T(8,128)S(1)}, f32[16,128,128]{2,1,0:T(8,128)}, u32[]{:S(2)}) %copy-start.4) | copy-done | bytes 1048600
  18.0 0.0 copy-start.6
  18.0 1.2 %copy-done.6 = f32[16,128,128]{2,1,0:T(8,128)S(1)} copy-done((f32[16,128,128]{2,1,0:T(8,128)S(1)}, f32[16,128,128]{2,1,0:T(8,128)}, u32[]{:S(2)}) %copy-start.6) | copy-done | bytes 1048600
  19.2 1.2 %copy-done.8 = f32[16,128,128]{2,1,0:T(8,128)S(1)} copy-done((f32[16,128,128]{2,1,0:T(8,128)S(1)}, f32[16,128,128]{2,1,0:T(8,128)}, u32[]{:S(2)}) %copy-start.8) | copy-done | bytes 1048600
  20.4 0.0 copy-start.7
  20.4 2.3 %edges.1 = (f32[96,128]{1,0:T(8,128)S(1)}, f32[80,128]{1,0:T(8,128)S(1)}, f32[96,128]{1,0:T(8,128)S(1)}, f32[80,128]{1,0:T(8,128)S(1)}, f32[4,16,128,128]{3,2,1,...) custom-call(f32[4,16,128,128]{3,2,1,0:T(8,128)S(1)} %copy-done, f32[16,128,128]{2,1,0:T(8,128)S(1)} %copy-done.4, ...), custom_call_target="tpu_custom_call" | custom-call | tf_op jit(solution)/shard_map/edges/pallas_call | solution.py:55
  22.7 0.0 copy-start.2
  22.7 2.0 %copy-done.2 = f32[4,16,128,128]{3,2,1,0:T(8,128)} copy-done((f32[4,16,128,128]{3,2,1,0:T(8,128)}, f32[4,16,128,128]{3,2,1,0:T(8,128)S(1)}, u32[]{:S(2)}) %copy-start.2) | copy-done | bytes 4194328
  24.8 1.0 %copy-done.9 = f32[16,128,128]{2,1,0:T(8,128)} copy-done((f32[16,128,128]{2,1,0:T(8,128)}, f32[16,128,128]{2,1,0:T(8,128)S(1)}, u32[]{:S(2)}) %copy-start.9) | copy-done | bytes 1048600
  25.8 1.0 %copy-done.11 = f32[16,128,128]{2,1,0:T(8,128)} copy-done((f32[16,128,128]{2,1,0:T(8,128)}, f32[16,128,128]{2,1,0:T(8,128)S(1)}, u32[]{:S(2)}) %copy-start.11) | copy-done | bytes 1048600
  26.7 3.5 %collective-permute-start = (f32[96,128]{1,0:T(8,128)S(1)}, f32[96,128]{1,0:T(8,128)S(1)}, u32[]{:S(2)}, u32[]{:S(2)}) collective-permute-start(f32[96,128]{1,0:T(8,128)S(1)} %get-tuple-element.65), channel_id=1, source_target_pairs={{0,8},{8,16},{16,24},{24,32},{32,40},{40,48},{48,56},{1,9},{9,17},... | collective-permute-start | bytes 147464 | tf_op jit(solution)/shard_map/ppermute | solution.py:320
  30.2 3.4 %collective-permute-start.2 = (f32[96,128]{1,0:T(8,128)S(1)}, f32[96,128]{1,0:T(8,128)S(1)}, u32[]{:S(2)}, u32[]{:S(2)}) collective-permute-start(f32[96,128]{1,0:T(8,128)S(1)} %get-tuple-element.67), channel_id=1, source_target_pairs={{0,1},{1,2},{2,3},{3,4},{4,5},{5,6},{6,7},{8,9},{9,10},{10,11},{11... | collective-permute-start | bytes 147464 | tf_op jit(solution)/shard_map/ppermute | solution.py:322
  33.6 1.3 %collective-permute-start.1 = (f32[80,128]{1,0:T(8,128)S(1)}, f32[80,128]{1,0:T(8,128)S(1)}, u32[]{:S(2)}, u32[]{:S(2)}) collective-permute-start(f32[80,128]{1,0:T(8,128)S(1)} %get-tuple-element.66), channel_id=1, source_target_pairs={{8,0},{16,8},{24,16},{32,24},{40,32},{48,40},{56,48},{9,1},{17,9},... | collective-permute-start | bytes 122888 | tf_op jit(solution)/shard_map/ppermute | solution.py:321
  34.9 1.3 %collective-permute-start.3 = (f32[80,128]{1,0:T(8,128)S(1)}, f32[80,128]{1,0:T(8,128)S(1)}, u32[]{:S(2)}, u32[]{:S(2)}) collective-permute-start(f32[80,128]{1,0:T(8,128)S(1)} %get-tuple-element.68), channel_id=1, source_target_pairs={{1,0},{2,1},{3,2},{4,3},{5,4},{6,5},{7,6},{9,8},{10,9},{11,10},{12... | collective-permute-start | bytes 122888 | tf_op jit(solution)/shard_map/ppermute | solution.py:323
  36.2 0.1 pad_add_fusion.1.origin_ref
  36.3 3.2 %collective-permute-done.1.he_ref = f32[80,128]{1,0:T(8,128)S(1)} collective-permute-done((f32[80,128]{1,0:T(8,128)S(1)}, f32[80,128]{1,0:T(8,128)S(1)}, u32[]{:S(2)}, u32[]{:S(2)}) %collective-permute-start.1) | collective-permute-done | bytes 40992 | tf_op jit(solution)/shard_map/ppermute | solution.py:321
  39.5 1.3 %collective-permute-done.3.hn_ref = f32[80,128]{1,0:T(8,128)S(1)} collective-permute-done((f32[80,128]{1,0:T(8,128)S(1)}, f32[80,128]{1,0:T(8,128)S(1)}, u32[]{:S(2)}, u32[]{:S(2)}) %collective-permute-start.3) | collective-permute-done | bytes 40992 | tf_op jit(solution)/shard_map/ppermute | solution.py:323
  40.8 0.0 collective-permute-done.hw_ref
  40.8 0.0 collective-permute-done.2.hs_ref
  40.8 0.0 copy-done.5
  40.8 0.0 copy-done.13
  40.8 0.0 copy-done.14
  40.8 0.0 copy-done.7
  40.8 0.0 copy-start.1
  40.8 2.2 %copy-done.1 = f32[4,16,128,128]{3,2,1,0:T(8,128)S(1)} copy-done((f32[4,16,128,128]{3,2,1,0:T(8,128)S(1)}, f32[4,16,128,128]{3,2,1,0:T(8,128)}, u32[]{:S(2)}) %copy-start.1) | copy-done | bytes 4194328
  43.0 2.2 %copy-done.3 = f32[4,16,128,128]{3,2,1,0:T(8,128)S(1)} copy-done((f32[4,16,128,128]{3,2,1,0:T(8,128)S(1)}, f32[4,16,128,128]{3,2,1,0:T(8,128)}, u32[]{:S(2)}) %copy-start.3) | copy-done | bytes 4194328
  45.2 1.2 %copy-done.10 = f32[16,128,128]{2,1,0:T(8,128)S(1)} copy-done((f32[16,128,128]{2,1,0:T(8,128)S(1)}, f32[16,128,128]{2,1,0:T(8,128)}, u32[]{:S(2)}) %copy-start.10) | copy-done | bytes 1048600
  46.4 1.2 %copy-done.12 = f32[16,128,128]{2,1,0:T(8,128)S(1)} copy-done((f32[16,128,128]{2,1,0:T(8,128)S(1)}, f32[16,128,128]{2,1,0:T(8,128)}, u32[]{:S(2)}) %copy-start.12) | copy-done | bytes 1048600
  47.6 7.4 %advance.1 = (f32[4,16,128,128]{3,2,1,0:T(8,128)}, bf16[512,2048]{1,0:T(8,128)(2,1)}) custom-call(s32[1]{0:T(128)} %bitcast.7.first_ref, f32[4,16,128,128]{3,2,1,0:T(8,128)S(1)} %copy-done.1, f32[4,16,128,128]{3,2,1,0:T(8,128)S(1)} %copy-done.3, f32[16,128,128]{2,1,0:T(8,128)S(1)} %copy-done.5, f32[16,128,128]{2,1,0:T(8,128)S(1)} %copy-done.10, ...), custom_call_target="tpu_custom_call" | custom-call | flops 41943040 | bytes 18874368 | tf_op jit(solution)/shard_map/advance/pallas_call | solution.py:137
  55.1 0.0 all-to-all-done.2
  55.1 7.3 %observe.2 = (f32[256,128]{1,0:T(8,128)}, s32[8,128]{1,0:T(8,128)S(1)}) custom-call(s32[2]{0:T(128)S(1)} %pad_add_fusion.1.origin_ref, f32[1536,128]{1,0:T(8,128)S(1)} %bitcast.34, bf16[512,2048]{1,0:T(8,128)(2,1)} %get-tuple-element.158.r_ref), custom_call_target="tpu_custom_call" | custom-call | tf_op jit(solution)/shard_map/observe/pallas_call | solution.py:292
  62.4 14.4 %all-to-all-start.3 = ((f32[64,4,128]{2,1,0:T(4,128)}), f32[64,4,128]{2,1,0:T(4,128)S(1)}, u32[]{:S(2)}, u32[]{:S(2)}) async-start(f32[64,4,128]{2,1,0:T(4,128)} %bitcast.15), calls=%async_computation.3 | async-start | bytes 262144 | tf_op jit(solution)/shard_map/all_to_all | solution.py:342
  76.8 0.6 slice.3
  78.1 8.5 %all-to-all-done.3 = f32[64,4,128]{2,1,0:T(4,128)S(1)} async-done(((f32[64,4,128]{2,1,0:T(4,128)}), f32[64,4,128]{2,1,0:T(4,128)S(1)}, u32[]{:S(2)}, u32[]{:S(2)}) %all-to-all-start.3) | async-done | bytes 131104 | tf_op jit(solution)/shard_map/all_to_all | solution.py:342
  86.6 0.1 reduce_sum.18
  86.7 0.0 copy-done.15
  86.7 0.0 copy-done.17
  86.7 0.0 copy-done.18
  86.7 0.0 copy-start.16
  86.8 0.6 copy-done.16
  (11 shorter events, 0.0 us)
Async XLA Ops:
  2.9 37.9 %copy-start.5 = (f32[16,128,128]{2,1,0:T(8,128)S(1)}, f32[16,128,128]{2,1,0:T(8,128)}, u32[]{:S(2)}) copy-start(f32[16,128,128]{2,1,0:T(8,128)} %we_ref.3) | copy-start | bytes 3145732
  2.9 37.9 %copy-start.13 = (f32[128,128]{1,0:T(8,128)S(1)}, f32[128,128]{1,0:T(8,128)}, u32[]{:S(2)}) copy-start(f32[128,128]{1,0:T(8,128)} %em_ref.1) | copy-start | bytes 196612
  2.9 37.9 %copy-start.14 = (s32[128,128]{1,0:T(8,128)S(1)}, s32[128,128]{1,0:T(8,128)}, u32[]{:S(2)}) copy-start(s32[128,128]{1,0:T(8,128)} %tag_ref.1) | copy-start | bytes 196612
  2.9 52.2 %all-to-all-start.2 = ((f32[64,24,128]{2,1,0:T(8,128)}), f32[64,24,128]{2,1,0:T(8,128)S(1)}, u32[]{:S(2)}, u32[]{:S(2)}) async-start(f32[64,24,128]{2,1,0:T(8,128)} %bitcast.13), calls=%async_computation.2 | async-start | bytes 1572864 | tf_op jit(solution)/shard_map/all_to_all | solution.py:338
  14.5 2.2 %copy-start = (f32[4,16,128,128]{3,2,1,0:T(8,128)S(1)}, f32[4,16,128,128]{3,2,1,0:T(8,128)}, u32[]{:S(2)}) copy-start(f32[4,16,128,128]{3,2,1,0:T(8,128)} %c_ref.3) | copy-start | bytes 12582916
  16.7 1.2 %copy-start.4 = (f32[16,128,128]{2,1,0:T(8,128)S(1)}, f32[16,128,128]{2,1,0:T(8,128)}, u32[]{:S(2)}) copy-start(f32[16,128,128]{2,1,0:T(8,128)} %we_ref.3) | copy-start | bytes 3145732
  18.0 1.2 %copy-start.6 = (f32[16,128,128]{2,1,0:T(8,128)S(1)}, f32[16,128,128]{2,1,0:T(8,128)}, u32[]{:S(2)}) copy-start(f32[16,128,128]{2,1,0:T(8,128)} %k_ref.3) | copy-start | bytes 3145732
  19.2 1.2 %copy-start.8 = (f32[16,128,128]{2,1,0:T(8,128)S(1)}, f32[16,128,128]{2,1,0:T(8,128)}, u32[]{:S(2)}) copy-start(f32[16,128,128]{2,1,0:T(8,128)} %wn_ref.1) | copy-start | bytes 3145732
  20.4 20.4 %copy-start.7 = (f32[16,128,128]{2,1,0:T(8,128)S(1)}, f32[16,128,128]{2,1,0:T(8,128)}, u32[]{:S(2)}) copy-start(f32[16,128,128]{2,1,0:T(8,128)} %k_ref.3) | copy-start | bytes 3145732
  22.7 2.0 %copy-start.2 = (f32[4,16,128,128]{3,2,1,0:T(8,128)}, f32[4,16,128,128]{3,2,1,0:T(8,128)S(1)}, u32[]{:S(2)}) copy-start(f32[4,16,128,128]{3,2,1,0:T(8,128)S(1)} %get-tuple-element.62.ct_ref) | copy-start | bytes 12582916
  24.7 1.0 %copy-start.9 = (f32[16,128,128]{2,1,0:T(8,128)}, f32[16,128,128]{2,1,0:T(8,128)S(1)}, u32[]{:S(2)}) copy-start(f32[16,128,128]{2,1,0:T(8,128)S(1)} %get-tuple-element.63.wnt_ref) | copy-start | bytes 3145732
  25.8 1.0 %copy-start.11 = (f32[16,128,128]{2,1,0:T(8,128)}, f32[16,128,128]{2,1,0:T(8,128)S(1)}, u32[]{:S(2)}) copy-start(f32[16,128,128]{2,1,0:T(8,128)S(1)} %get-tuple-element.64.kt_ref) | copy-start | bytes 3145732
  26.7 14.1 %collective-permute-start = (f32[96,128]{1,0:T(8,128)S(1)}, f32[96,128]{1,0:T(8,128)S(1)}, u32[]{:S(2)}, u32[]{:S(2)}) collective-permute-start(f32[96,128]{1,0:T(8,128)S(1)} %get-tuple-element.65), channel_id=1, source_target_pairs={{0,8},{8,16},{16,24},{24,32},{32,40},{40,48},{48,56},{1,9},{9,17},... | collective-permute-start | bytes 147464 | tf_op jit(solution)/shard_map/ppermute | solution.py:320
  30.2 10.6 %collective-permute-start.2 = (f32[96,128]{1,0:T(8,128)S(1)}, f32[96,128]{1,0:T(8,128)S(1)}, u32[]{:S(2)}, u32[]{:S(2)}) collective-permute-start(f32[96,128]{1,0:T(8,128)S(1)} %get-tuple-element.67), channel_id=1, source_target_pairs={{0,1},{1,2},{2,3},{3,4},{4,5},{5,6},{6,7},{8,9},{9,10},{10,11},{11... | collective-permute-start | bytes 147464 | tf_op jit(solution)/shard_map/ppermute | solution.py:322
  33.6 5.9 %collective-permute-start.1 = (f32[80,128]{1,0:T(8,128)S(1)}, f32[80,128]{1,0:T(8,128)S(1)}, u32[]{:S(2)}, u32[]{:S(2)}) collective-permute-start(f32[80,128]{1,0:T(8,128)S(1)} %get-tuple-element.66), channel_id=1, source_target_pairs={{8,0},{16,8},{24,16},{32,24},{40,32},{48,40},{56,48},{9,1},{17,9},... | collective-permute-start | bytes 122888 | tf_op jit(solution)/shard_map/ppermute | solution.py:321
  34.9 5.9 %collective-permute-start.3 = (f32[80,128]{1,0:T(8,128)S(1)}, f32[80,128]{1,0:T(8,128)S(1)}, u32[]{:S(2)}, u32[]{:S(2)}) collective-permute-start(f32[80,128]{1,0:T(8,128)S(1)} %get-tuple-element.68), channel_id=1, source_target_pairs={{1,0},{2,1},{3,2},{4,3},{5,4},{6,5},{7,6},{9,8},{10,9},{11,10},{12... | collective-permute-start | bytes 122888 | tf_op jit(solution)/shard_map/ppermute | solution.py:323
  40.8 2.2 %copy-start.1 = (f32[4,16,128,128]{3,2,1,0:T(8,128)S(1)}, f32[4,16,128,128]{3,2,1,0:T(8,128)}, u32[]{:S(2)}) copy-start(f32[4,16,128,128]{3,2,1,0:T(8,128)} %c_ref.3) | copy-start | bytes 12582916
  43.0 2.2 %copy-start.3 = (f32[4,16,128,128]{3,2,1,0:T(8,128)S(1)}, f32[4,16,128,128]{3,2,1,0:T(8,128)}, u32[]{:S(2)}) copy-start(f32[4,16,128,128]{3,2,1,0:T(8,128)} %copy-done.2) | copy-start | bytes 12582916
  45.2 1.2 %copy-start.10 = (f32[16,128,128]{2,1,0:T(8,128)S(1)}, f32[16,128,128]{2,1,0:T(8,128)}, u32[]{:S(2)}) copy-start(f32[16,128,128]{2,1,0:T(8,128)} %copy-done.9) | copy-start | bytes 3145732
  46.4 1.2 %copy-start.12 = (f32[16,128,128]{2,1,0:T(8,128)S(1)}, f32[16,128,128]{2,1,0:T(8,128)}, u32[]{:S(2)}) copy-start(f32[16,128,128]{2,1,0:T(8,128)} %copy-done.11) | copy-start | bytes 3145732
  47.6 39.1 %copy-start.15 = (f32[128,80]{0,1:T(8,128)S(1)}, f32[128,80]{0,1:T(8,128)}, u32[]{:S(2)}) copy-start(f32[128,80]{0,1:T(8,128)} %param.17) | copy-start | bytes 122884
  47.6 39.1 %copy-start.17 = (s32[128,2]{0,1:T(2,128)S(1)}, s32[128,2]{0,1:T(2,128)}, u32[]{:S(2)}) copy-start(s32[128,2]{0,1:T(2,128)} %param.18) | copy-start | bytes 3076
  47.6 39.1 %copy-start.18 = (s32[64]{0:T(128)S(1)}, s32[64]{0:T(128)}, u32[]{:S(2)}) copy-start(s32[64]{0:T(128)} %owner_ref.1) | copy-start | bytes 772
  62.4 24.3 %all-to-all-start.3 = ((f32[64,4,128]{2,1,0:T(4,128)}), f32[64,4,128]{2,1,0:T(4,128)S(1)}, u32[]{:S(2)}, u32[]{:S(2)}) async-start(f32[64,4,128]{2,1,0:T(4,128)} %bitcast.15), calls=%async_computation.3 | async-start | bytes 262144 | tf_op jit(solution)/shard_map/all_to_all | solution.py:342
  86.7 0.6 copy-start.16

commit v3 on v2

v3 whole, which is shorter than its diff:
```python
import functools
import math

import jax
import jax.numpy as jnp
from jax import lax
from jax.experimental import pallas as pl
from jax.experimental.pallas import tpu as pltpu
from jax.sharding import PartitionSpec as P

FP = 32
CAP = 24
LANES = 128
CHUNK = 256
VMEM_ALL = 56 << 20
VMEM_MOST = 52 << 20
TILES = ("gx", "gy")


def pack_kernel(
    tiles_x, tiles_y, size, nz, number_ref, owner_ref, fp_ref, corner_ref, out_ref, m_ref
):
    tiles = tiles_x * tiles_y
    obs = fp_ref.shape[1]
    width = 2 * FP + nz
    tile = lax.broadcasted_iota(jnp.int32, (tiles, obs), 0)
    first_x = (tile // tiles_y) * size[0]
    first_y = (tile % tiles_y) * size[1]
    x0 = corner_ref[0:1, :]
    y0 = corner_ref[1:2, :]
    touch = (
        (x0 < first_x + size[0])
        & (x0 + FP > first_x)
        & (y0 < first_y + size[1])
        & (y0 + FP > first_y)
    )
    ones = jnp.where(touch, 1.0, 0.0)
    earlier = lax.broadcasted_iota(jnp.int32, (obs, obs), 0) < lax.broadcasted_iota(
        jnp.int32, (obs, obs), 1
    )
    rank = jnp.dot(
        ones.astype(jnp.bfloat16),
        jnp.where(earlier, 1.0, 0.0).astype(jnp.bfloat16),
        preferred_element_type=jnp.float32,
    ).astype(jnp.int32)
    count = jnp.sum(ones, axis=1, keepdims=True)
    most = jnp.max(count, axis=0, keepdims=True)
    now = jnp.clip(count - (number_ref[0] * CAP).astype(jnp.float32), 0.0, CAP)
    slot = jnp.where(touch, rank - number_ref[0] * CAP, -1)
    which = lax.broadcasted_iota(jnp.int32, (tiles, CAP, obs), 1)
    pick = jnp.where(slot[:, None, :] == which, 1.0, 0.0).reshape(tiles * CAP, obs)
    pick = pick.astype(jnp.bfloat16)

    def rotated(profile, by):
        shift = 1
        while shift < FP:
            turn = (by & shift) != 0
            profile = jnp.where(turn, pltpu.roll(profile, shift, 0), profile)
            shift *= 2
        return profile

    m_ref[0:FP, :] = rotated(fp_ref[0:FP, :], x0)
    m_ref[FP : 2 * FP, :] = rotated(fp_ref[FP : 2 * FP, :], y0)
    m_ref[2 * FP : width, :] = fp_ref[2 * FP : width, :]
    m_ref[width:, :] = jnp.zeros_like(m_ref[width:, :])
    m_ref[width : width + 2, :] = corner_ref[...].astype(jnp.float32)
    m_ref[width + 2 : width + 3, :] = lax.broadcasted_iota(jnp.int32, (1, obs), 1).astype(
        jnp.float32
    )
    rows = m_ref[...].T
    lane = lax.broadcasted_iota(jnp.int32, rows.shape, 1)
    high = rows.astype(jnp.bfloat16)
    low = jnp.where(lane < 2 * FP, 0.0, rows - high.astype(jnp.float32)).astype(jnp.bfloat16)
    packed = jnp.dot(pick, high, preferred_element_type=jnp.float32) + jnp.dot(
        pick, low, preferred_element_type=jnp.float32
    )
    lane = lax.broadcasted_iota(jnp.int32, packed.shape, 1)
    packed = jnp.where(lane == width + 3, most, packed)
    owner = owner_ref[number_ref[1]].astype(jnp.float32)
    packed = jnp.where(lane == width + 4, owner, packed)
    now = jnp.broadcast_to(now[:, :, None], (tiles, CAP, LANES)).reshape(packed.shape)
    out_ref[...] = jnp.where(lane == width + 5, now, packed)


def pack(number, owner_map, footprint, corners, tiles_x, tiles_y, size):
    obs, width = footprint.shape
    nz = width - 2 * FP
    tiles = tiles_x * tiles_y
    vmem = pl.BlockSpec(memory_space=pltpu.VMEM)
    smem = pl.BlockSpec(memory_space=pltpu.SMEM)
    return pl.pallas_call(
        functools.partial(pack_kernel, tiles_x, tiles_y, size, nz),
        in_specs=[smem, smem, vmem, vmem],
        out_specs=vmem,
        out_shape=jax.ShapeDtypeStruct((tiles * CAP, LANES), jnp.float32),
        scratch_shapes=[pltpu.VMEM((LANES, obs), jnp.float32)],
        compiler_params=pltpu.CompilerParams(vmem_limit_bytes=VMEM_ALL),
        name="pack",
    )(number, owner_map, footprint.T, corners.T)


def prepare_kernel(
    tiles_x, tiles_y, size, nz, zb, number_ref, owner_ref, fp_ref, corner_ref,
    c_hbm, we_hbm, wn_hbm, k_hbm, sent_ref, e_ref, w_ref, n_ref, s_ref,
    m_ref, c_ref, we_ref, wn_ref, k_ref, sems,
):
    count, cols_x, cols_y = c_ref.shape[0], c_ref.shape[2], c_ref.shape[3]

    def fetch(i):
        at = pl.ds(i * zb, zb)
        return (
            pltpu.make_async_copy(c_hbm.at[:, at], c_ref.at[:, at], sems.at[0, i]),
            pltpu.make_async_copy(k_hbm.at[at], k_ref.at[at], sems.at[1, i]),
            pltpu.make_async_copy(wn_hbm.at[at], wn_ref.at[at], sems.at[2, i]),
            pltpu.make_async_copy(
                we_hbm.at[at, cols_x - 8 : cols_x], we_ref.at[at], sems.at[3, i]
            ),
        )

    for i in range(nz // zb):
        for copy in fetch(i):
            copy.start()

    pack_kernel(
        tiles_x, tiles_y, size, nz, number_ref, owner_ref, fp_ref, corner_ref, sent_ref, m_ref
    )

    def ends(slot, a_ref):
        e_ref[pl.ds(slot, 1), :] = a_ref[cols_x - 1 : cols_x, :]
        w_ref[pl.ds(slot, 1), :] = a_ref[0:1, :]
        flipped = a_ref[...].T
        n_ref[pl.ds(slot, 1), :] = flipped[cols_y - 1 : cols_y, :]
        s_ref[pl.ds(slot, 1), :] = flipped[0:1, :]

    def body(i, carry):
        for copy in fetch(i):
            copy.wait()
        for zi in range(zb):
            z = i * zb + zi
            for t in range(count):
                ends(t * nz + z, c_ref.at[t, z])
            ends(count * nz + z, k_ref.at[z])
            slot = (count + 1) * nz + z
            e_ref[pl.ds(slot, 1), :] = we_ref[z, 7:8, :]
            n_ref[pl.ds(slot, 1), :] = wn_ref[z].T[cols_y - 1 : cols_y, :]
        return carry

    lax.fori_loop(0, nz // zb, body, 0)


def prepare(
    number, owner_map, footprint, corners, tiles_x, tiles_y,
    tracers, wind_east, wind_north, diffusivity,
):
    count, nz, cols_x, cols_y = tracers.shape
    obs = footprint.shape[0]
    zb = 4
    f32 = jnp.float32
    flat = [(count + 2, cols_y), (count + 1, cols_y), (count + 2, cols_x), (count + 1, cols_x)]
    vmem = pl.BlockSpec(memory_space=pltpu.VMEM)
    smem = pl.BlockSpec(memory_space=pltpu.SMEM)
    return pl.pallas_call(
        functools.partial(prepare_kernel, tiles_x, tiles_y, (cols_x, cols_y), nz, zb),
        in_specs=[smem, smem, vmem, vmem, *[pl.BlockSpec(memory_space=pl.ANY)] * 4],
        out_specs=[vmem] * 5,
        out_shape=[
            jax.ShapeDtypeStruct((tiles_x * tiles_y * CAP, LANES), f32),
            *[jax.ShapeDtypeStruct((n * nz, width), f32) for n, width in flat],
        ],
        scratch_shapes=[
            pltpu.VMEM((LANES, obs), f32),
            pltpu.VMEM(tracers.shape, f32),
            pltpu.VMEM((nz, 8, cols_y), f32),
            pltpu.VMEM(wind_north.shape, f32),
            pltpu.VMEM(diffusivity.shape, f32),
            pltpu.SemaphoreType.DMA((4, nz // zb)),
        ],
        compiler_params=pltpu.CompilerParams(vmem_limit_bytes=VMEM_ALL),
        name="prepare",
    )(
        number, owner_map, footprint.T, corners.T, tracers, wind_east, wind_north, diffusivity
    )


def observe_kernel(nz, count, origin_ref, rows_ref, r_ref, out_ref, most_ref, near_ref, w_ref):
    cols = LANES
    chunk = w_ref.shape[1]
    scale = 1.0 / (FP * math.sqrt(nz))
    width = 2 * FP + nz
    lines = out_ref.shape[0]
    sources = rows_ref.shape[0] // CAP
    out_ref[...] = jnp.zeros_like(out_ref)
    heads = rows_ref[pl.ds(0, sources, stride=CAP), :]
    most = jnp.max(heads, axis=0, keepdims=True)
    most_ref[...] = jnp.broadcast_to(most, most_ref.shape).astype(jnp.int32)

    filled = 0
    for b in range(sources):
        near_ref[pl.ds(filled, CAP), :] = rows_ref[b * CAP : (b + 1) * CAP, :]
        filled += heads[b, width + 5].astype(jnp.int32)
    near_ref[pl.ds(filled, chunk), :] = jnp.zeros((chunk, LANES), jnp.float32)

    def body(step, carry):
        rows = near_ref[pl.ds(pl.multiple_of(step * chunk, chunk), chunk), :].T
        place = lax.broadcasted_iota(jnp.int32, (cols, chunk), 0)

        def along(profile, corner, origin):
            offset = place - (corner.astype(jnp.int32) - origin)
            inside = (offset >= 0) & (offset < FP)
            return jnp.where(inside, jnp.concatenate([profile] * (cols // FP), axis=0), 0.0)

        wy = along(rows[FP : 2 * FP], rows[width + 1 : width + 2], origin_ref[1])
        for z in range(nz):
            part = wy * rows[2 * FP + z : 2 * FP + z + 1]
            w_ref[z * cols : (z + 1) * cols, :] = part.astype(jnp.bfloat16)
        got = jnp.dot(r_ref[...], w_ref[...], preferred_element_type=jnp.float32)
        wx = along(rows[0:FP], rows[width : width + 1], origin_ref[0]) * scale
        values = [
            jnp.sum(got[t * cols : (t + 1) * cols] * wx, axis=0, keepdims=True)
            for t in range(count)
        ]
        values = jnp.concatenate(values * (8 // count), axis=0)
        owner = lax.broadcasted_iota(jnp.int32, (lines, chunk), 0) // count
        mine = owner == rows[width + 4 : width + 5].astype(jnp.int32)
        spread = jnp.where(mine, jnp.concatenate([values] * (lines // 8), axis=0), 0.0)
        high = spread.astype(jnp.bfloat16)
        low = (spread - high.astype(jnp.float32)).astype(jnp.bfloat16)
        obs = jnp.where(place == rows[width + 2 : width + 3].astype(jnp.int32), 1.0, 0.0)
        obs = obs.astype(jnp.bfloat16)
        across = (((1,), (1,)), ((), ()))
        out_ref[...] += lax.dot_general(
            high, obs, across, preferred_element_type=jnp.float32
        ) + lax.dot_general(low, obs, across, preferred_element_type=jnp.float32)
        return carry

    lax.fori_loop(0, (filled + chunk - 1) // chunk, body, 0)


def observe_scratch(rows, rounded_shape):
    return [
        pltpu.VMEM((rows + CHUNK, LANES), jnp.float32),
        pltpu.VMEM((rounded_shape[1], CHUNK), jnp.bfloat16),
    ]


def observed_shapes(sources, count):
    return [
        jax.ShapeDtypeStruct((sources * count, LANES), jnp.float32),
        jax.ShapeDtypeStruct((8, LANES), jnp.int32),
    ]


def observe(origin, rows, rounded, count, nz, sources):
    vmem = pl.BlockSpec(memory_space=pltpu.VMEM)
    smem = pl.BlockSpec(memory_space=pltpu.SMEM)
    return pl.pallas_call(
        functools.partial(observe_kernel, nz, count),
        in_specs=[smem, vmem, vmem],
        out_specs=[vmem, vmem],
        out_shape=observed_shapes(sources, count),
        scratch_shapes=observe_scratch(rows.shape[0], rounded.shape),
        compiler_params=pltpu.CompilerParams(vmem_limit_bytes=VMEM_MOST),
        name="observe",
    )(origin, rows, rounded)


PAD = 8


def step_kernel(
    nz, zb, place_ref, c_hbm, we_hbm, wn_hbm, k_hbm, em_ref, tag_ref,
    hw_ref, he_ref, hs_ref, hn_ref, rows_ref, out_hbm, r_hbm, parts_ref, most_ref,
    c_ref, we_ref, wn_ref, k_ref, ct_ref, wnt_ref, kt_ref, y_ref, out_ref, r_ref,
    near_ref, weight_ref, sems, out_sems, r_sem,
):
    count, _, cols_x, cols_y = c_hbm.shape
    slab = 32
    in_x, in_y = pl.ds(PAD, cols_x), pl.ds(PAD, cols_y)

    def fetch(i):
        at = pl.ds(i * zb, zb)
        return (
            pltpu.make_async_copy(c_hbm.at[:, at], c_ref.at[:, at, in_x], sems.at[0, i]),
            pltpu.make_async_copy(k_hbm.at[at], k_ref.at[at, in_x], sems.at[1, i]),
            pltpu.make_async_copy(we_hbm.at[at], we_ref.at[at, in_x], sems.at[2, i]),
            pltpu.make_async_copy(wn_hbm.at[at], wn_ref.at[at], sems.at[3, i]),
        )

    def send(i):
        at = pl.ds(i * zb, zb)
        return pltpu.make_async_copy(out_ref.at[:, at], out_hbm.at[:, at], out_sems.at[i])

    for i in range(nz // zb):
        for copy in fetch(i):
            copy.start()

    def surround(a_ref, low_ref, high_ref, slot):
        last = a_ref.shape[0] - PAD
        a_ref[PAD - 1 : PAD, :] = low_ref[pl.ds(slot, 1), :]
        if high_ref is not None:
            a_ref[last : last + 1, :] = high_ref[pl.ds(slot, 1), :]

    def three(a_ref, at):
        first = PAD + at
        return (
            a_ref[first : first + slab, :],
            a_ref[first + 1 : first + 1 + slab, :],
            a_ref[first - 1 : first - 1 + slab, :],
        )

    def coefficients(wind_ref, k_ref, at):
        wind, _, wind_m = three(wind_ref, at)
        k, k_p, k_m = three(k_ref, at)
        mix, mix_m = 0.5 * (k + k_p), 0.5 * (k + k_m)
        own = jnp.maximum(wind, 0.0) + mix - (jnp.minimum(wind_m, 0.0) - mix_m)
        return own, mix - jnp.minimum(wind, 0.0), jnp.maximum(wind_m, 0.0) + mix_m

    def body(i, carry):
        for copy in fetch(i):
            copy.wait()
        for zi in range(zb):
            z = i * zb + zi
            at_k, at_w = count * nz + z, (count + 1) * nz + z
            surround(k_ref.at[z], hw_ref, he_ref, at_k)
            surround(we_ref.at[z], hw_ref, None, at_w)
            kt_ref[zi, PAD : PAD + cols_y, :] = k_ref[z, PAD : PAD + cols_x, :].T
            surround(kt_ref.at[zi], hs_ref, hn_ref, at_k)
            wnt_ref[zi, PAD : PAD + cols_y, :] = wn_ref[z].T
            surround(wnt_ref.at[zi], hs_ref, None, at_w)
            for t in range(count):
                surround(c_ref.at[t, z], hw_ref, he_ref, t * nz + z)
                ct_ref[t, zi, PAD : PAD + cols_y, :] = c_ref[t, z, PAD : PAD + cols_x, :].T
                surround(ct_ref.at[t, zi], hs_ref, hn_ref, t * nz + z)
            for at in range(0, cols_y, slab):
                own, up, down = coefficients(wnt_ref.at[zi], kt_ref.at[zi], at)
                for t in range(count):
                    c, c_p, c_m = three(ct_ref.at[t, zi], at)
                    y_ref[t, zi, at : at + slab, :] = up * c_p + down * c_m - own * c
            for t in range(count):
                y_ref[t, zi] = y_ref[t, zi].T
            lanes = pl.ds(pl.multiple_of(z * cols_y, cols_y), cols_y)
            for at in range(0, cols_x, slab):
                own, up, down = coefficients(we_ref.at[z], k_ref.at[z], at)
                own = 1.0 - own
                rows = slice(at, at + slab)
                for t in range(count):
                    c, c_p, c_m = three(c_ref.at[t, z], at)
                    new = own * c + up * c_p + down * c_m + y_ref[t, zi, rows, :]
                    if zi == 0:
                        hit = (tag_ref[rows, :] == place_ref[2] + t) & (i == 0)
                        new = new + jnp.where(hit, em_ref[rows, :], 0.0)
                    out_ref[t, z, rows, :] = new
                    r_ref[t * cols_x + at : t * cols_x + at + slab, lanes] = new.astype(
                        jnp.bfloat16
                    )
        send(i).start()
        return carry

    lax.fori_loop(0, nz // zb, body, 0)
    keep = pltpu.make_async_copy(r_ref, r_hbm, r_sem)
    keep.start()
    observe_kernel(
        nz, count, place_ref, rows_ref, r_ref, parts_ref, most_ref, near_ref, weight_ref
    )
    for i in range(nz // zb):
        send(i).wait()
    keep.wait()


def advance(place, tracers, wind_east, wind_north, k, emission, tag, halos, rows, sources):
    count, nz, cols_x, cols_y = tracers.shape
    zb = 4
    f32 = jnp.float32
    vmem = pl.BlockSpec(memory_space=pltpu.VMEM)
    hbm = pl.BlockSpec(memory_space=pl.ANY)
    rounded = jax.ShapeDtypeStruct((count * cols_x, nz * cols_y), jnp.bfloat16)
    return pl.pallas_call(
        functools.partial(step_kernel, nz, zb),
        in_specs=[pl.BlockSpec(memory_space=pltpu.SMEM), *[hbm] * 4, *[vmem] * 7],
        out_specs=[hbm, hbm, vmem, vmem],
        out_shape=[
            jax.ShapeDtypeStruct(tracers.shape, f32),
            rounded,
            *observed_shapes(sources, count),
        ],
        scratch_shapes=[
            pltpu.VMEM((count, nz, cols_x + 2 * PAD, cols_y), f32),
            pltpu.VMEM((nz, cols_x + 2 * PAD, cols_y), f32),
            pltpu.VMEM((nz, cols_x, cols_y), f32),
            pltpu.VMEM((nz, cols_x + 2 * PAD, cols_y), f32),
            pltpu.VMEM((count, zb, cols_y + 2 * PAD, cols_x), f32),
            pltpu.VMEM((zb, cols_y + 2 * PAD, cols_x), f32),
            pltpu.VMEM((zb, cols_y + 2 * PAD, cols_x), f32),
            pltpu.VMEM((count, zb, cols_y, cols_x), f32),
            pltpu.VMEM(tracers.shape, f32),
            pltpu.VMEM(rounded.shape, rounded.dtype),
            *observe_scratch(rows.shape[0], rounded.shape),
            pltpu.SemaphoreType.DMA((4, nz // zb)),
            pltpu.SemaphoreType.DMA((nz // zb,)),
            pltpu.SemaphoreType.DMA,
        ],
        cost_estimate=pl.CostEstimate(
            flops=40 * tracers.size, bytes_accessed=13 << 20, transcendentals=0
        ),
        compiler_params=pltpu.CompilerParams(vmem_limit_bytes=VMEM_MOST),
        name="advance",
    )(place, tracers, wind_east, wind_north, k, emission, tag, *halos, rows)


def per_device(
    tracers, wind_east, wind_north, diffusivity, emission, region_tag, footprint, corners, owner_map
):
    count, nz, cols_x, cols_y = tracers.shape
    tiles_x, tiles_y = lax.axis_size("gx"), lax.axis_size("gy")
    tiles = tiles_x * tiles_y
    obs = footprint.shape[0]
    me = lax.axis_index(TILES)
    place = [lax.axis_index("gx") * cols_x, lax.axis_index("gy") * cols_y]
    place = jnp.stack([*place, lax.axis_index("tracer") * count]).astype(jnp.int32)

    def numbered(number):
        return jnp.stack([number, me]).astype(jnp.int32)

    sent, east, west, north, south = prepare(
        numbered(jnp.int32(0)), owner_map, footprint, corners, tiles_x, tiles_y,
        tracers, wind_east, wind_north, diffusivity,
    )

    def to_tiles(rows):
        rows = lax.all_to_all(rows.reshape(tiles, CAP, LANES), TILES, 0, 0)
        return rows.reshape(tiles * CAP, LANES)

    def to_owners(parts):
        return jnp.sum(lax.all_to_all(parts.reshape(tiles, count, obs), TILES, 0, 0), axis=0)

    rows = to_tiles(sent)
    up_x = [(i, i + 1) for i in range(tiles_x - 1)]
    up_y = [(i, i + 1) for i in range(tiles_y - 1)]
    halos = (
        lax.ppermute(east, "gx", up_x),
        lax.ppermute(west, "gx", [(b, a) for a, b in up_x]),
        lax.ppermute(north, "gy", up_y),
        lax.ppermute(south, "gy", [(b, a) for a, b in up_y]),
    )
    stepped, rounded, parts, most = advance(
        place, tracers, wind_east, wind_north, diffusivity, emission, region_tag, halos, rows, tiles
    )
    observed = to_owners(parts)

    def later_round(number, total):
        rows = to_tiles(
            pack(
                numbered(number), owner_map, footprint, corners, tiles_x, tiles_y, (cols_x, cols_y)
            )
        )
        parts, _ = observe(place, rows, rounded, count, nz, tiles)
        return total + to_owners(parts)

    rounds = (most[0, 2 * FP + nz + 3] + CAP - 1) // CAP
    observed = lax.fori_loop(jnp.int32(1), rounds, later_round, observed)
    return (stepped, observed)


def solution(mesh):
    return jax.shard_map(
        per_device,
        mesh=mesh,
        in_specs=(
            P("tracer", None, "gx", "gy"),
            P(None, "gx", "gy"),
            P(None, "gx", "gy"),
            P(None, "gx", "gy"),
            P("gx", "gy"),
            P("gx", "gy"),
            P(("gx", "gy"), None),
            P(("gx", "gy"), None),
            P(),
        ),
        out_specs=(P("tracer", None, "gx", "gy"), P("tracer", ("gx", "gy"))),
        check_vma=False,
    )
```

time: 88.1 us -> 68.1 us (0.77)
  local copies, waits for them, and re-layouts: 17.8 us -> 1.21 us
  Pallas kernels: 19.2 us -> 13.3 us
  starting transfers between devices: 35.5 us -> 38.7 us
    unnamed x38 -> x12, local copies, waits for them, and re-layouts: 17.2 us -> 0.59 us
    pallas_call x4 -> x2, Pallas kernels: 19.2 us -> 13.3 us  [the longest x1 8.39 us: advance(): pl.pallas_call(functools.partial(step_kernel, nz, zb), in_specs=[pl.Block...]
    ppermute x1, waiting for transfers between devices: 3.21 us -> 0.01 us  [per_device(): lax.ppermute(west, 'gx', [(b, a) for a, b in up_x])]
    ppermute x1, waiting for transfers between devices: 0.01 us -> 1.95 us  [per_device(): lax.ppermute(north, 'gy', up_y)]
    all_to_all x2, waiting for transfers between devices: 8.49 us -> 10.4 us  [the longest x1 8.53 us: to_owners(): lax.all_to_all(parts.reshape(tiles, count, obs), TILES, 0, 0)]
    ppermute x1, waiting for transfers between devices: 1.3 us -> 0.01 us  [per_device(): lax.ppermute(south, 'gy', [(b, a) for a, b in up_y])]
    ppermute x1, starting transfers between devices: 3.37 us -> 4.55 us  [per_device(): lax.ppermute(north, 'gy', up_y)]
    ppermute x1, starting transfers between devices: 3.47 us -> 4.55 us  [per_device(): lax.ppermute(east, 'gx', up_x)]
  transfers between devices with their start and end apart: 6 -> 6, of which waited for: 3 -> 3; matrix products, arithmetic and copies ran while one was open for 1% -> 1% of each run, Pallas kernels for 11% -> 0%
where the time goes in v3:
time: 68.1 us; the launch traced here: 67.7 us
  starting transfers between devices  38.7 us (57%)
  Pallas kernels  13.3 us (20%)
  waiting for transfers between devices  12.4 us (18%)
  between operations  1.42 us (2%)
  local copies, waits for them, and re-layouts  1.21 us (2%)
  other arithmetic  0.74 us (1%)
    all_to_all x1, starting transfers between devices, to_owners(): lax.all_to_all(parts.reshape(tiles, count, obs), TILES, 0, 0)  15.5 us
    all_to_all x1, starting transfers between devices, to_tiles(): rows = lax.all_to_all(rows.reshape(tiles, CAP, LANES), TILES, 0, 0)  11.5 us
    all_to_all x1, waiting for transfers between devices, to_owners(): lax.all_to_all(parts.reshape(tiles, count, obs), TILES, 0, 0)  8.53 us
    pallas_call x1, Pallas kernels, advance(): pl.pallas_call(functools.partial(step_kernel, nz, zb), in_specs=[pl.Block...  8.39 us
    pallas_call x1, Pallas kernels, prepare(): pl.pallas_call(functools.partial(prepare_kernel, tiles_x, tiles_y, (cols_...  4.96 us
    ppermute x1, starting transfers between devices, per_device(): lax.ppermute(east, 'gx', up_x)  4.55 us
    ppermute x1, starting transfers between devices, per_device(): lax.ppermute(north, 'gy', up_y)  4.55 us
    ppermute x1, waiting for transfers between devices, per_device(): lax.ppermute(north, 'gy', up_y)  1.95 us
  transfers between devices with their start and end apart: 6, of which 3 were waited for; matrix products, arithmetic and copies ran while one was open for 1% of the time, Pallas kernels for 0%

profile of v3, /device:TPU:0, one launch (start us, length us, event | category | flops | bytes accessed | tf_op | source)
XLA Modules:
  0.0 67.7 jit_solution(9388475452675164265)
XLA Ops:
  0.6 0.6 pad_add_fusion.2.number_ref
  1.2 0.0 copy-start
  1.2 0.0 copy-start.1
  1.2 5.0 %prepare.1 = (f32[1536,128]{1,0:T(8,128)}, f32[96,128]{1,0:T(8,128)}, f32[80,128]{1,0:T(8,128)}, f32[96,128]{1,0:T(8,128)}, f32[80,128]{1,0:T(8,128)}) custom-call(s32[2]{0:T(128)} %pad_add_fusion.2.number_ref, s32[64]{0:T(128)} %owner_ref.1, f32[80,128]{1,0:T(8,128)} %bitcast.35, s32[2,128]{1,0:T(2,128)} %bitcast.38, f32[4,16,128,128]{3,2,1,0:T(8,128)} %c_hbm.3, ...), custom_call_target="tpu_custom_call" | custom-call | tf_op jit(solution)/shard_map/prepare/pallas_call | solution.py:162
  6.2 11.5 %all-to-all-start.2 = ((f32[64,24,128]{2,1,0:T(8,128)}), f32[64,24,128]{2,1,0:T(8,128)S(1)}, u32[]{:S(2)}, u32[]{:S(2)}) async-start(f32[64,24,128]{2,1,0:T(8,128)} %bitcast.37), calls=%async_computation.2 | async-start | bytes 1572864 | tf_op jit(solution)/shard_map/all_to_all | solution.py:430
  17.7 1.3 %collective-permute-start.1 = (f32[80,128]{1,0:T(8,128)}, f32[80,128]{1,0:T(8,128)S(1)}, u32[]{:S(2)}, u32[]{:S(2)}) collective-permute-start(f32[80,128]{1,0:T(8,128)} %get-tuple-element.61), channel_id=1, source_target_pairs={{8,0},{16,8},{24,16},{32,24},{40,32},{48,40},{56,48},{9,1},{17,9},... | collective-permute-start | bytes 122888 | tf_op jit(solution)/shard_map/ppermute | solution.py:441
  19.0 1.3 %collective-permute-start.3 = (f32[80,128]{1,0:T(8,128)}, f32[80,128]{1,0:T(8,128)S(1)}, u32[]{:S(2)}, u32[]{:S(2)}) collective-permute-start(f32[80,128]{1,0:T(8,128)} %get-tuple-element.63), channel_id=1, source_target_pairs={{1,0},{2,1},{3,2},{4,3},{5,4},{6,5},{7,6},{9,8},{10,9},{11,10},{12... | collective-permute-start | bytes 122888 | tf_op jit(solution)/shard_map/ppermute | solution.py:443
  20.3 4.5 %collective-permute-start = (f32[96,128]{1,0:T(8,128)}, f32[96,128]{1,0:T(8,128)S(1)}, u32[]{:S(2)}, u32[]{:S(2)}) collective-permute-start(f32[96,128]{1,0:T(8,128)} %get-tuple-element.60), channel_id=1, source_target_pairs={{0,8},{8,16},{16,24},{24,32},{32,40},{40,48},{48,56},{1,9},{9,17},... | collective-permute-start | bytes 147464 | tf_op jit(solution)/shard_map/ppermute | solution.py:440
  24.9 4.5 %collective-permute-start.2 = (f32[96,128]{1,0:T(8,128)}, f32[96,128]{1,0:T(8,128)S(1)}, u32[]{:S(2)}, u32[]{:S(2)}) collective-permute-start(f32[96,128]{1,0:T(8,128)} %get-tuple-element.62), channel_id=1, source_target_pairs={{0,1},{1,2},{2,3},{3,4},{4,5},{5,6},{6,7},{8,9},{9,10},{10,11},{11... | collective-permute-start | bytes 147464 | tf_op jit(solution)/shard_map/ppermute | solution.py:442
  29.4 0.1 pad_add_fusion.1.place_ref
  29.5 0.0 collective-permute-done.1.he_ref
  29.5 0.0 collective-permute-done.3.hn_ref
  29.5 0.0 collective-permute-done.hw_ref
  29.5 1.9 %collective-permute-done.2.hs_ref = f32[96,128]{1,0:T(8,128)S(1)} collective-permute-done((f32[96,128]{1,0:T(8,128)}, f32[96,128]{1,0:T(8,128)S(1)}, u32[]{:S(2)}, u32[]{:S(2)}) %collective-permute-start.2) | collective-permute-done | bytes 49184 | tf_op jit(solution)/shard_map/ppermute | solution.py:442
  31.5 1.9 %all-to-all-done.2 = f32[64,24,128]{2,1,0:T(8,128)S(1)} async-done(((f32[64,24,128]{2,1,0:T(8,128)}), f32[64,24,128]{2,1,0:T(8,128)S(1)}, u32[]{:S(2)}, u32[]{:S(2)}) %all-to-all-start.2) | async-done | bytes 786464 | tf_op jit(solution)/shard_map/all_to_all | solution.py:430
  33.4 0.0 copy-done
  33.4 0.0 copy-done.1
  33.4 0.0 copy-start.2
  33.4 0.0 copy-start.4
  33.4 0.0 copy-start.5
  33.4 8.4 %advance.1 = (f32[4,16,128,128]{3,2,1,0:T(8,128)}, bf16[512,2048]{1,0:T(8,128)(2,1)S(1)}, f32[256,128]{1,0:T(8,128)}, s32[8,128]{1,0:T(8,128)S(1)}) custom-call(s32[3]{0:T(128)S(1)} %pad_add_fusion.1.place_ref, f32[4,16,128,128]{3,2,1,0:T(8,128)} %c_hbm.3, f32[16,128,128]{2,1,0:T(8,128)} %we_hbm.3, f32[16,128,128]{2,1,0:T(8,128)} %wn_hbm.3, ...), custom_call_target="tpu_custom_call" | custom-call | flops 41943040 | bytes 13631488 | tf_op jit(solution)/shard_map/advance/pallas_call | solution.py:377
  41.8 15.5 %all-to-all-start.3 = ((f32[64,4,128]{2,1,0:T(4,128)}), f32[64,4,128]{2,1,0:T(4,128)S(1)}, u32[]{:S(2)}, u32[]{:S(2)}) async-start(f32[64,4,128]{2,1,0:T(4,128)} %bitcast.15), calls=%async_computation.3 | async-start | bytes 262144 | tf_op jit(solution)/shard_map/all_to_all | solution.py:434
  57.2 0.6 slice.3
  58.5 8.5 %all-to-all-done.3 = f32[64,4,128]{2,1,0:T(4,128)S(1)} async-done(((f32[64,4,128]{2,1,0:T(4,128)}), f32[64,4,128]{2,1,0:T(4,128)S(1)}, u32[]{:S(2)}, u32[]{:S(2)}) %all-to-all-start.3) | async-done | bytes 131104 | tf_op jit(solution)/shard_map/all_to_all | solution.py:434
  67.0 0.1 reduce_sum.18
  67.1 0.0 copy-done.2
  67.1 0.0 copy-done.4
  67.1 0.0 copy-done.5
  67.2 0.0 copy-start.3
  67.2 0.6 copy-done.3
  (1 shorter events, 0.0 us)
Async XLA Ops:
  1.2 32.1 %copy-start = (f32[128,128]{1,0:T(8,128)S(1)}, f32[128,128]{1,0:T(8,128)}, u32[]{:S(2)}) copy-start(f32[128,128]{1,0:T(8,128)} %em_ref.1) | copy-start | bytes 196612
  1.2 32.1 %copy-start.1 = (s32[128,128]{1,0:T(8,128)S(1)}, s32[128,128]{1,0:T(8,128)}, u32[]{:S(2)}) copy-start(s32[128,128]{1,0:T(8,128)} %tag_ref.1) | copy-start | bytes 196612
  6.2 27.2 %all-to-all-start.2 = ((f32[64,24,128]{2,1,0:T(8,128)}), f32[64,24,128]{2,1,0:T(8,128)S(1)}, u32[]{:S(2)}, u32[]{:S(2)}) async-start(f32[64,24,128]{2,1,0:T(8,128)} %bitcast.37), calls=%async_computation.2 | async-start | bytes 1572864 | tf_op jit(solution)/shard_map/all_to_all | solution.py:430
  17.7 11.8 %collective-permute-start.1 = (f32[80,128]{1,0:T(8,128)}, f32[80,128]{1,0:T(8,128)S(1)}, u32[]{:S(2)}, u32[]{:S(2)}) collective-permute-start(f32[80,128]{1,0:T(8,128)} %get-tuple-element.61), channel_id=1, source_target_pairs={{8,0},{16,8},{24,16},{32,24},{40,32},{48,40},{56,48},{9,1},{17,9},... | collective-permute-start | bytes 122888 | tf_op jit(solution)/shard_map/ppermute | solution.py:441
  19.0 10.5 %collective-permute-start.3 = (f32[80,128]{1,0:T(8,128)}, f32[80,128]{1,0:T(8,128)S(1)}, u32[]{:S(2)}, u32[]{:S(2)}) collective-permute-start(f32[80,128]{1,0:T(8,128)} %get-tuple-element.63), channel_id=1, source_target_pairs={{1,0},{2,1},{3,2},{4,3},{5,4},{6,5},{7,6},{9,8},{10,9},{11,10},{12... | collective-permute-start | bytes 122888 | tf_op jit(solution)/shard_map/ppermute | solution.py:443
  20.3 9.2 %collective-permute-start = (f32[96,128]{1,0:T(8,128)}, f32[96,128]{1,0:T(8,128)S(1)}, u32[]{:S(2)}, u32[]{:S(2)}) collective-permute-start(f32[96,128]{1,0:T(8,128)} %get-tuple-element.60), channel_id=1, source_target_pairs={{0,8},{8,16},{16,24},{24,32},{32,40},{40,48},{48,56},{1,9},{9,17},... | collective-permute-start | bytes 147464 | tf_op jit(solution)/shard_map/ppermute | solution.py:440
  24.9 6.6 %collective-permute-start.2 = (f32[96,128]{1,0:T(8,128)}, f32[96,128]{1,0:T(8,128)S(1)}, u32[]{:S(2)}, u32[]{:S(2)}) collective-permute-start(f32[96,128]{1,0:T(8,128)} %get-tuple-element.62), channel_id=1, source_target_pairs={{0,1},{1,2},{2,3},{3,4},{4,5},{5,6},{6,7},{8,9},{9,10},{10,11},{11... | collective-permute-start | bytes 147464 | tf_op jit(solution)/shard_map/ppermute | solution.py:442
  33.4 33.8 %copy-start.2 = (f32[128,80]{0,1:T(8,128)S(1)}, f32[128,80]{0,1:T(8,128)}, u32[]{:S(2)}) copy-start(f32[128,80]{0,1:T(8,128)} %param.17) | copy-start | bytes 122884
  33.4 33.8 %copy-start.4 = (s32[128,2]{0,1:T(2,128)S(1)}, s32[128,2]{0,1:T(2,128)}, u32[]{:S(2)}) copy-start(s32[128,2]{0,1:T(2,128)} %param.18) | copy-start | bytes 3076
  33.4 33.8 %copy-start.5 = (s32[64]{0:T(128)S(1)}, s32[64]{0:T(128)}, u32[]{:S(2)}) copy-start(s32[64]{0:T(128)} %owner_ref.1) | copy-start | bytes 772
  41.8 25.3 %all-to-all-start.3 = ((f32[64,4,128]{2,1,0:T(4,128)}), f32[64,4,128]{2,1,0:T(4,128)S(1)}, u32[]{:S(2)}, u32[]{:S(2)}) async-start(f32[64,4,128]{2,1,0:T(4,128)} %bitcast.15), calls=%async_computation.3 | async-start | bytes 262144 | tf_op jit(solution)/shard_map/all_to_all | solution.py:434
  67.2 0.6 copy-start.3

commit v4 on v3

--- a/solution.py
+++ b/solution.py
@@ -13,12 +13,12 @@
 LANES = 128
 CHUNK = 256
 VMEM_ALL = 56 << 20
-VMEM_MOST = 52 << 20
+VMEM_MOST = 50 << 20
 TILES = ("gx", "gy")
 
 
 def pack_kernel(
-    tiles_x, tiles_y, size, nz, number_ref, owner_ref, fp_ref, corner_ref, out_ref, m_ref
+    tiles_x, tiles_y, size, nz, number_ref, me_ref, owner_ref, fp_ref, corner_ref, out_ref, m_ref
 ):
     tiles = tiles_x * tiles_y
     obs = fp_ref.shape[1]
@@ -76,13 +76,13 @@
     )
     lane = lax.broadcasted_iota(jnp.int32, packed.shape, 1)
     packed = jnp.where(lane == width + 3, most, packed)
-    owner = owner_ref[number_ref[1]].astype(jnp.float32)
+    owner = owner_ref[me_ref[0]].astype(jnp.float32)
     packed = jnp.where(lane == width + 4, owner, packed)
     now = jnp.broadcast_to(now[:, :, None], (tiles, CAP, LANES)).reshape(packed.shape)
     out_ref[...] = jnp.where(lane == width + 5, now, packed)
 
 
-def pack(number, owner_map, footprint, corners, tiles_x, tiles_y, size):
+def pack(number, me, owner_map, footprint, corners, tiles_x, tiles_y, size):
     obs, width = footprint.shape
     nz = width - 2 * FP
     tiles = tiles_x * tiles_y
@@ -90,18 +90,18 @@
     smem = pl.BlockSpec(memory_space=pltpu.SMEM)
     return pl.pallas_call(
         functools.partial(pack_kernel, tiles_x, tiles_y, size, nz),
-        in_specs=[smem, smem, vmem, vmem],
+        in_specs=[smem, smem, smem, vmem, vmem],
         out_specs=vmem,
         out_shape=jax.ShapeDtypeStruct((tiles * CAP, LANES), jnp.float32),
         scratch_shapes=[pltpu.VMEM((LANES, obs), jnp.float32)],
         compiler_params=pltpu.CompilerParams(vmem_limit_bytes=VMEM_ALL),
         name="pack",
-    )(number, owner_map, footprint.T, corners.T)
+    )(number, me, owner_map, footprint.T, corners.T)
 
 
 def prepare_kernel(
-    tiles_x, tiles_y, size, nz, zb, number_ref, owner_ref, fp_ref, corner_ref,
-    c_hbm, we_hbm, wn_hbm, k_hbm, sent_ref, e_ref, w_ref, n_ref, s_ref,
+    tiles_x, tiles_y, size, nz, zb, number_ref, me_ref, owner_ref, fp_ref, corner_ref,
+    c_hbm, we_hbm, wn_hbm, k_hbm, sent_ref, xa_ref, xb_ref, ya_ref, yb_ref,
     m_ref, c_ref, we_ref, wn_ref, k_ref, sems,
 ):
     count, cols_x, cols_y = c_ref.shape[0], c_ref.shape[2], c_ref.shape[3]
@@ -122,15 +122,21 @@
             copy.start()
 
     pack_kernel(
-        tiles_x, tiles_y, size, nz, number_ref, owner_ref, fp_ref, corner_ref, sent_ref, m_ref
-    )
+        tiles_x, tiles_y, size, nz, number_ref, me_ref, owner_ref, fp_ref, corner_ref, sent_ref, m_ref
+    )
+
+    even_x = (me_ref[0] // tiles_y) % 2 == 0
+    even_y = (me_ref[0] % tiles_y) % 2 == 0
+    row_a = jnp.where(even_x, cols_x - 1, 0)
+    row_b = cols_x - 1 - row_a
 
     def ends(slot, a_ref):
-        e_ref[pl.ds(slot, 1), :] = a_ref[cols_x - 1 : cols_x, :]
-        w_ref[pl.ds(slot, 1), :] = a_ref[0:1, :]
+        xa_ref[pl.ds(slot, 1), :] = a_ref[pl.ds(row_a, 1), :]
+        xb_ref[pl.ds(slot, 1), :] = a_ref[pl.ds(row_b, 1), :]
         flipped = a_ref[...].T
-        n_ref[pl.ds(slot, 1), :] = flipped[cols_y - 1 : cols_y, :]
-        s_ref[pl.ds(slot, 1), :] = flipped[0:1, :]
+        low, high = flipped[0:1, :], flipped[cols_y - 1 : cols_y, :]
+        ya_ref[pl.ds(slot, 1), :] = jnp.where(even_y, high, low)
+        yb_ref[pl.ds(slot, 1), :] = jnp.where(even_y, low, high)
 
     def body(i, carry):
         for copy in fetch(i):
@@ -141,31 +147,34 @@
                 ends(t * nz + z, c_ref.at[t, z])
             ends(count * nz + z, k_ref.at[z])
             slot = (count + 1) * nz + z
-            e_ref[pl.ds(slot, 1), :] = we_ref[z, 7:8, :]
-            n_ref[pl.ds(slot, 1), :] = wn_ref[z].T[cols_y - 1 : cols_y, :]
+            for to_ref in (xa_ref, xb_ref):
+                to_ref[pl.ds(slot, 1), :] = we_ref[z, 7:8, :]
+            last = wn_ref[z].T[cols_y - 1 : cols_y, :]
+            for to_ref in (ya_ref, yb_ref):
+                to_ref[pl.ds(slot, 1), :] = last
         return carry
 
     lax.fori_loop(0, nz // zb, body, 0)
 
 
 def prepare(
-    number, owner_map, footprint, corners, tiles_x, tiles_y,
+    number, me, owner_map, footprint, corners, tiles_x, tiles_y,
     tracers, wind_east, wind_north, diffusivity,
 ):
     count, nz, cols_x, cols_y = tracers.shape
     obs = footprint.shape[0]
     zb = 4
     f32 = jnp.float32
-    flat = [(count + 2, cols_y), (count + 1, cols_y), (count + 2, cols_x), (count + 1, cols_x)]
+    edge_rows = (count + 2) * nz
     vmem = pl.BlockSpec(memory_space=pltpu.VMEM)
     smem = pl.BlockSpec(memory_space=pltpu.SMEM)
     return pl.pallas_call(
         functools.partial(prepare_kernel, tiles_x, tiles_y, (cols_x, cols_y), nz, zb),
-        in_specs=[smem, smem, vmem, vmem, *[pl.BlockSpec(memory_space=pl.ANY)] * 4],
+        in_specs=[smem, smem, smem, vmem, vmem, *[pl.BlockSpec(memory_space=pl.ANY)] * 4],
         out_specs=[vmem] * 5,
         out_shape=[
             jax.ShapeDtypeStruct((tiles_x * tiles_y * CAP, LANES), f32),
-            *[jax.ShapeDtypeStruct((n * nz, width), f32) for n, width in flat],
+            *[jax.ShapeDtypeStruct((edge_rows, width), f32) for width in (cols_y, cols_y, cols_x, cols_x)],
         ],
         scratch_shapes=[
             pltpu.VMEM((LANES, obs), f32),
@@ -178,7 +187,7 @@
         compiler_params=pltpu.CompilerParams(vmem_limit_bytes=VMEM_ALL),
         name="prepare",
     )(
-        number, owner_map, footprint.T, corners.T, tracers, wind_east, wind_north, diffusivity
+        number, me, owner_map, footprint.T, corners.T, tracers, wind_east, wind_north, diffusivity
     )
 
 
@@ -269,9 +278,9 @@
 
 def step_kernel(
     nz, zb, place_ref, c_hbm, we_hbm, wn_hbm, k_hbm, em_ref, tag_ref,
-    hw_ref, he_ref, hs_ref, hn_ref, rows_ref, out_hbm, r_hbm, parts_ref, most_ref,
+    yb_ref, ya_ref, xb_ref, xa_ref, rows_ref, out_hbm, r_hbm, parts_ref, most_ref,
     c_ref, we_ref, wn_ref, k_ref, ct_ref, wnt_ref, kt_ref, y_ref, out_ref, r_ref,
-    near_ref, weight_ref, sems, out_sems, r_sem,
+    halo_x_ref, halo_y_ref, near_ref, weight_ref, sems, out_sems, r_sem,
 ):
     count, _, cols_x, cols_y = c_hbm.shape
     slab = 32
@@ -293,6 +302,15 @@
     for i in range(nz // zb):
         for copy in fetch(i):
             copy.start()
+
+    side_x = 1 - (place_ref[0] // cols_x) % 2
+    side_y = 1 - (place_ref[1] // cols_y) % 2
+    halo_x_ref[side_x] = xa_ref[...]
+    halo_x_ref[1 - side_x] = xb_ref[...]
+    halo_y_ref[side_y] = ya_ref[...]
+    halo_y_ref[1 - side_y] = yb_ref[...]
+    hw_ref, he_ref = halo_x_ref.at[0], halo_x_ref.at[1]
+    hs_ref, hn_ref = halo_y_ref.at[0], halo_y_ref.at[1]
 
     def surround(a_ref, low_ref, high_ref, slot):
         last = a_ref.shape[0] - PAD
@@ -394,6 +412,8 @@
             pltpu.VMEM((count, zb, cols_y, cols_x), f32),
             pltpu.VMEM(tracers.shape, f32),
             pltpu.VMEM(rounded.shape, rounded.dtype),
+            pltpu.VMEM((2, *halos[0].shape), f32),
+            pltpu.VMEM((2, *halos[2].shape), f32),
             *observe_scratch(rows.shape[0], rounded.shape),
             pltpu.SemaphoreType.DMA((4, nz // zb)),
             pltpu.SemaphoreType.DMA((nz // zb,)),
@@ -414,15 +434,12 @@
     tiles_x, tiles_y = lax.axis_size("gx"), lax.axis_size("gy")
     tiles = tiles_x * tiles_y
     obs = footprint.shape[0]
-    me = lax.axis_index(TILES)
+    me = lax.axis_index(TILES).astype(jnp.int32).reshape(1)
     place = [lax.axis_index("gx") * cols_x, lax.axis_index("gy") * cols_y]
     place = jnp.stack([*place, lax.axis_index("tracer") * count]).astype(jnp.int32)
 
-    def numbered(number):
-        return jnp.stack([number, me]).astype(jnp.int32)
-
-    sent, east, west, north, south = prepare(
-        numbered(jnp.int32(0)), owner_map, footprint, corners, tiles_x, tiles_y,
+    sent, *edges = prepare(
+        jnp.zeros((1,), jnp.int32), me, owner_map, footprint, corners, tiles_x, tiles_y,
         tracers, wind_east, wind_north, diffusivity,
     )
 
@@ -434,13 +451,13 @@
         return jnp.sum(lax.all_to_all(parts.reshape(tiles, count, obs), TILES, 0, 0), axis=0)
 
     rows = to_tiles(sent)
-    up_x = [(i, i + 1) for i in range(tiles_x - 1)]
-    up_y = [(i, i + 1) for i in range(tiles_y - 1)]
+    def swap(edge, axis, first):
+        pairs = [(i, i + 1) for i in range(first, lax.axis_size(axis) - 1, 2)]
+        return lax.ppermute(edge, axis, pairs + [(b, a) for a, b in pairs])
+
+    edge_xa, edge_xb, edge_ya, edge_yb = edges
     halos = (
-        lax.ppermute(east, "gx", up_x),
-        lax.ppermute(west, "gx", [(b, a) for a, b in up_x]),
-        lax.ppermute(north, "gy", up_y),
-        lax.ppermute(south, "gy", [(b, a) for a, b in up_y]),
+        swap(edge_yb, "gy", 1), swap(edge_ya, "gy", 0), swap(edge_xb, "gx", 1), swap(edge_xa, "gx", 0)
     )
     stepped, rounded, parts, most = advance(
         place, tracers, wind_east, wind_north, diffusivity, emission, region_tag, halos, rows, tiles
@@ -450,7 +467,7 @@
     def later_round(number, total):
         rows = to_tiles(
             pack(
-                numbered(number), owner_map, footprint, corners, tiles_x, tiles_y, (cols_x, cols_y)
+                number.reshape(1), me, owner_map, footprint, corners, tiles_x, tiles_y, (cols_x, cols_y)
             )
         )
         parts, _ = observe(place, rows, rounded, count, nz, tiles)

time: 68.1 us -> 60.1 us (0.88)
  starting transfers between devices: 38.7 us -> 29.3 us
  waiting for transfers between devices: 12.4 us -> 13.9 us
    all_to_all x1, starting transfers between devices: 15.5 us -> 7.9 us  [to_owners(): lax.all_to_all(parts.reshape(tiles, count, obs), TILES, 0, 0)]
    ppermute x4, starting transfers between devices: 11.7 us -> 9.93 us  [swap(): return lax.ppermute(edge, axis, pairs + [(b, a) for a, b in pairs])]
    all_to_all x1, waiting for transfers between devices: 1.88 us -> 2.87 us  [to_tiles(): rows = lax.all_to_all(rows.reshape(tiles, CAP, LANES), TILES, 0, 0)]
where the time goes in v4:
time: 60.1 us; the launch traced here: 59.7 us
  starting transfers between devices  29.3 us (49%)
  waiting for transfers between devices  13.9 us (23%)
  Pallas kernels  13.5 us (22%)
  between operations  1.51 us (3%)
  local copies, waits for them, and re-layouts  1.27 us (2%)
    all_to_all x1, starting transfers between devices, to_tiles(): rows = lax.all_to_all(rows.reshape(tiles, CAP, LANES), TILES, 0, 0)  11.5 us
    ppermute x4, starting transfers between devices, swap(): return lax.ppermute(edge, axis, pairs + [(b, a) for a, b in pairs])  9.93 us
    all_to_all x1, waiting for transfers between devices, to_owners(): lax.all_to_all(parts.reshape(tiles, count, obs), TILES, 0, 0)  8.42 us
    pallas_call x1, Pallas kernels, advance(): pl.pallas_call(functools.partial(step_kernel, nz, zb), in_specs=[pl.Block...  8.31 us
    all_to_all x1, starting transfers between devices, to_owners(): lax.all_to_all(parts.reshape(tiles, count, obs), TILES, 0, 0)  7.9 us
    pallas_call x1, Pallas kernels, prepare(): pl.pallas_call(functools.partial(prepare_kernel, tiles_x, tiles_y, (cols_...  5.22 us
    all_to_all x1, waiting for transfers between devices, to_tiles(): rows = lax.all_to_all(rows.reshape(tiles, CAP, LANES), TILES, 0, 0)  2.87 us
    ppermute x4, waiting for transfers between devices, swap(): return lax.ppermute(edge, axis, pairs + [(b, a) for a, b in pairs])  2.62 us
  transfers between devices with their start and end apart: 6, of which 3 were waited for; matrix products, arithmetic and copies ran while one was open for 1% of the time, Pallas kernels for 0%

profile of v4, /device:TPU:0, one launch (start us, length us, event | category | flops | bytes accessed | tf_op | source)
XLA Modules:
  0.0 59.7 jit_solution(9921142843253571085)
XLA Ops:
  0.6 0.0 copy-start
  0.6 0.0 copy-start.1
  0.7 0.0 copy-start.2
  0.7 0.0 copy-start.3
  0.7 5.2 %prepare.1 = (f32[1536,128]{1,0:T(8,128)}, f32[96,128]{1,0:T(8,128)}, f32[96,128]{1,0:T(8,128)}, f32[96,128]{1,0:T(8,128)}, f32[96,128]{1,0:T(8,128)}) custom-call(s32[1]{0:T(128)} %constant.39.clone.1.number_ref, s32[1]{0:T(128)} %bitcast.9.me_ref, s32[64]{0:T(128)} %owner_ref.1, f32[80,128]{1,0:T(8,128)} %bitcast.32, s32[2,128]{1,0:T(2,128)} %bitcast.35, ...), custom_call_target="tpu_custom_call" | custom-call | tf_op jit(solution)/shard_map/prepare/pallas_call | solution.py:171
  5.9 11.5 %all-to-all-start.2 = ((f32[64,24,128]{2,1,0:T(8,128)}), f32[64,24,128]{2,1,0:T(8,128)S(1)}, u32[]{:S(2)}, u32[]{:S(2)}) async-start(f32[64,24,128]{2,1,0:T(8,128)} %bitcast.34), calls=%async_computation.2 | async-start | bytes 1572864 | tf_op jit(solution)/shard_map/all_to_all | solution.py:447
  17.4 0.7 %collective-permute-start = (f32[96,128]{1,0:T(8,128)}, f32[96,128]{1,0:T(8,128)S(1)}, u32[]{:S(2)}, u32[]{:S(2)}) collective-permute-start(f32[96,128]{1,0:T(8,128)} %get-tuple-element.60), channel_id=1, source_target_pairs={{1,2},{3,4},{5,6},{2,1},{4,3},{6,5},{9,10},{11,12},{13,14},{10,9},... | collective-permute-start | bytes 147464 | tf_op jit(solution)/shard_map/ppermute | solution.py:456
  18.1 4.4 %collective-permute-start.1 = (f32[96,128]{1,0:T(8,128)}, f32[96,128]{1,0:T(8,128)S(1)}, u32[]{:S(2)}, u32[]{:S(2)}) collective-permute-start(f32[96,128]{1,0:T(8,128)} %get-tuple-element.61), channel_id=1, source_target_pairs={{0,1},{2,3},{4,5},{6,7},{1,0},{3,2},{5,4},{7,6},{8,9},{10,11},{12,... | collective-permute-start | bytes 147464 | tf_op jit(solution)/shard_map/ppermute | solution.py:456
  22.5 0.7 %collective-permute-start.2 = (f32[96,128]{1,0:T(8,128)}, f32[96,128]{1,0:T(8,128)S(1)}, u32[]{:S(2)}, u32[]{:S(2)}) collective-permute-start(f32[96,128]{1,0:T(8,128)} %get-tuple-element.62), channel_id=1, source_target_pairs={{8,16},{24,32},{40,48},{16,8},{32,24},{48,40},{9,17},{25,33},{41,4... | collective-permute-start | bytes 147464 | tf_op jit(solution)/shard_map/ppermute | solution.py:456
  23.1 4.3 %collective-permute-start.3 = (f32[96,128]{1,0:T(8,128)}, f32[96,128]{1,0:T(8,128)S(1)}, u32[]{:S(2)}, u32[]{:S(2)}) collective-permute-start(f32[96,128]{1,0:T(8,128)} %get-tuple-element.63), channel_id=1, source_target_pairs={{0,8},{16,24},{32,40},{48,56},{8,0},{24,16},{40,32},{56,48},{1,9},... | collective-permute-start | bytes 147464 | tf_op jit(solution)/shard_map/ppermute | solution.py:456
  27.4 0.1 pad_add_fusion.place_ref
  27.4 0.0 collective-permute-done.yb_ref
  27.4 0.0 collective-permute-done.1.ya_ref
  27.5 0.0 collective-permute-done.2.xb_ref
  27.5 2.6 %collective-permute-done.3.xa_ref = f32[96,128]{1,0:T(8,128)S(1)} collective-permute-done((f32[96,128]{1,0:T(8,128)}, f32[96,128]{1,0:T(8,128)S(1)}, u32[]{:S(2)}, u32[]{:S(2)}) %collective-permute-start.3) | collective-permute-done | bytes 49184 | tf_op jit(solution)/shard_map/ppermute | solution.py:456
  30.1 2.9 %all-to-all-done.2 = f32[64,24,128]{2,1,0:T(8,128)S(1)} async-done(((f32[64,24,128]{2,1,0:T(8,128)}), f32[64,24,128]{2,1,0:T(8,128)S(1)}, u32[]{:S(2)}, u32[]{:S(2)}) %all-to-all-start.2) | async-done | bytes 786464 | tf_op jit(solution)/shard_map/all_to_all | solution.py:447
  32.9 0.0 copy-done
  32.9 0.0 copy-done.1
  32.9 0.0 copy-done.2
  33.0 0.0 copy-done.3
  33.0 0.0 copy-start.4
  33.0 0.0 copy-start.6
  33.0 0.0 copy-start.7
  33.0 8.3 %advance.1 = (f32[4,16,128,128]{3,2,1,0:T(8,128)}, bf16[512,2048]{1,0:T(8,128)(2,1)}, f32[256,128]{1,0:T(8,128)}, s32[8,128]{1,0:T(8,128)S(1)}) custom-call(s32[3]{0:T(128)S(1)} %pad_add_fusion.place_ref, f32[4,16,128,128]{3,2,1,0:T(8,128)} %c_hbm.3, f32[16,128,128]{2,1,0:T(8,128)S(1)} %copy-done, f32[16,128,128]{2,1,0:T(8,128)S(1)} %copy-done.1, ...), custom_call_target="tpu_custom_call" | custom-call | flops 41943040 | bytes 13631488 | tf_op jit(solution)/shard_map/advance/pallas_call | solution.py:395
  41.3 7.9 %all-to-all-start.3 = ((f32[64,4,128]{2,1,0:T(4,128)}), f32[64,4,128]{2,1,0:T(4,128)S(1)}, u32[]{:S(2)}, u32[]{:S(2)}) async-start(f32[64,4,128]{2,1,0:T(4,128)} %bitcast.14), calls=%async_computation.3 | async-start | bytes 262144 | tf_op jit(solution)/shard_map/all_to_all | solution.py:451
  49.2 0.7 %slice.3 = s32[1,1]{1,0:T(1,128)} slice(s32[8,128]{1,0:T(8,128)S(1)} %get-tuple-element.67), slice={[0:1], [83:84]} | slice | bytes 8 | tf_op jit(solution)/shard_map/slice | solution.py:476
  50.6 8.4 %all-to-all-done.3 = f32[64,4,128]{2,1,0:T(4,128)S(1)} async-done(((f32[64,4,128]{2,1,0:T(4,128)}), f32[64,4,128]{2,1,0:T(4,128)S(1)}, u32[]{:S(2)}, u32[]{:S(2)}) %all-to-all-start.3) | async-done | bytes 131104 | tf_op jit(solution)/shard_map/all_to_all | solution.py:451
  59.0 0.1 reduce_sum.18
  59.1 0.0 copy-done.4
  59.1 0.0 copy-done.6
  59.1 0.0 copy-done.7
  59.1 0.0 copy-start.5
  59.2 0.6 copy-done.5
  (1 shorter events, 0.0 us)
Async XLA Ops:
  0.6 32.3 %copy-start = (f32[16,128,128]{2,1,0:T(8,128)S(1)}, f32[16,128,128]{2,1,0:T(8,128)}, u32[]{:S(2)}) copy-start(f32[16,128,128]{2,1,0:T(8,128)} %we_hbm.3) | copy-start | bytes 3145732
  0.6 32.3 %copy-start.1 = (f32[16,128,128]{2,1,0:T(8,128)S(1)}, f32[16,128,128]{2,1,0:T(8,128)}, u32[]{:S(2)}) copy-start(f32[16,128,128]{2,1,0:T(8,128)} %wn_hbm.3) | copy-start | bytes 3145732
  0.7 32.3 %copy-start.2 = (f32[128,128]{1,0:T(8,128)S(1)}, f32[128,128]{1,0:T(8,128)}, u32[]{:S(2)}) copy-start(f32[128,128]{1,0:T(8,128)} %em_ref.1) | copy-start | bytes 196612
  0.7 32.3 %copy-start.3 = (s32[128,128]{1,0:T(8,128)S(1)}, s32[128,128]{1,0:T(8,128)}, u32[]{:S(2)}) copy-start(s32[128,128]{1,0:T(8,128)} %tag_ref.1) | copy-start | bytes 196612
  5.9 27.0 %all-to-all-start.2 = ((f32[64,24,128]{2,1,0:T(8,128)}), f32[64,24,128]{2,1,0:T(8,128)S(1)}, u32[]{:S(2)}, u32[]{:S(2)}) async-start(f32[64,24,128]{2,1,0:T(8,128)} %bitcast.34), calls=%async_computation.2 | async-start | bytes 1572864 | tf_op jit(solution)/shard_map/all_to_all | solution.py:447
  17.4 10.0 %collective-permute-start = (f32[96,128]{1,0:T(8,128)}, f32[96,128]{1,0:T(8,128)S(1)}, u32[]{:S(2)}, u32[]{:S(2)}) collective-permute-start(f32[96,128]{1,0:T(8,128)} %get-tuple-element.60), channel_id=1, source_target_pairs={{1,2},{3,4},{5,6},{2,1},{4,3},{6,5},{9,10},{11,12},{13,14},{10,9},... | collective-permute-start | bytes 147464 | tf_op jit(solution)/shard_map/ppermute | solution.py:456
  18.1 9.4 %collective-permute-start.1 = (f32[96,128]{1,0:T(8,128)}, f32[96,128]{1,0:T(8,128)S(1)}, u32[]{:S(2)}, u32[]{:S(2)}) collective-permute-start(f32[96,128]{1,0:T(8,128)} %get-tuple-element.61), channel_id=1, source_target_pairs={{0,1},{2,3},{4,5},{6,7},{1,0},{3,2},{5,4},{7,6},{8,9},{10,11},{12,... | collective-permute-start | bytes 147464 | tf_op jit(solution)/shard_map/ppermute | solution.py:456
  22.5 5.0 %collective-permute-start.2 = (f32[96,128]{1,0:T(8,128)}, f32[96,128]{1,0:T(8,128)S(1)}, u32[]{:S(2)}, u32[]{:S(2)}) collective-permute-start(f32[96,128]{1,0:T(8,128)} %get-tuple-element.62), channel_id=1, source_target_pairs={{8,16},{24,32},{40,48},{16,8},{32,24},{48,40},{9,17},{25,33},{41,4... | collective-permute-start | bytes 147464 | tf_op jit(solution)/shard_map/ppermute | solution.py:456
  23.1 7.0 %collective-permute-start.3 = (f32[96,128]{1,0:T(8,128)}, f32[96,128]{1,0:T(8,128)S(1)}, u32[]{:S(2)}, u32[]{:S(2)}) collective-permute-start(f32[96,128]{1,0:T(8,128)} %get-tuple-element.63), channel_id=1, source_target_pairs={{0,8},{16,24},{32,40},{48,56},{8,0},{24,16},{40,32},{56,48},{1,9},... | collective-permute-start | bytes 147464 | tf_op jit(solution)/shard_map/ppermute | solution.py:456
  33.0 26.1 %copy-start.4 = (f32[128,80]{0,1:T(8,128)S(1)}, f32[128,80]{0,1:T(8,128)}, u32[]{:S(2)}) copy-start(f32[128,80]{0,1:T(8,128)} %param.17) | copy-start | bytes 122884
  33.0 26.1 %copy-start.6 = (s32[128,2]{0,1:T(2,128)S(1)}, s32[128,2]{0,1:T(2,128)}, u32[]{:S(2)}) copy-start(s32[128,2]{0,1:T(2,128)} %param.18) | copy-start | bytes 3076
  33.0 26.1 %copy-start.7 = (s32[64]{0:T(128)S(1)}, s32[64]{0:T(128)}, u32[]{:S(2)}) copy-start(s32[64]{0:T(128)} %owner_ref.1) | copy-start | bytes 772
  41.3 17.7 %all-to-all-start.3 = ((f32[64,4,128]{2,1,0:T(4,128)}), f32[64,4,128]{2,1,0:T(4,128)S(1)}, u32[]{:S(2)}, u32[]{:S(2)}) async-start(f32[64,4,128]{2,1,0:T(4,128)} %bitcast.14), calls=%async_computation.3 | async-start | bytes 262144 | tf_op jit(solution)/shard_map/all_to_all | solution.py:451
  59.1 0.6 copy-start.5
